TPU v7x, 32 devices: a whole 2x2x4 slice. The times are simulated.
32 devices in a mesh: section: 4 (over z), head: 8 (over y, x, core).
Axes of the slice: x: 2, y: 2, z: 4, core: 2. Of those that a mesh axis runs over, the one named last changes fastest.
Arguments:
- hidden_in: bfloat16 [12288, 2048], P(('section', 'head')), may hold values from -3 to 3
- norm_gain: float32 [2048], replicated, may hold values from 0.1 to 1.9
- w_qkv: bfloat16 [2048, 3, 2048], P(None, None, 'head'), may hold values from -0.5 to 0.5
- w_out: bfloat16 [2048, 2048], P('head'), may hold values from -0.375 to 0.375
- block_lists: int32 [24, 12], P('section'), may hold values from -1 to 23, as said below
Outputs:
- mixed: bfloat16 [12288, 2048], P(('section', 'head'))
Inputs may be any that keep to these rules, and one draw needn't show every extreme that they name: `block_lists`: row b starts with b itself, then holds 1 + b * 11 // 23 - 1 further distinct blocks below b, then -1 in every remaining slot.
All inputs are finite; a program needn't handle non-finite values.
Results may differ from a plain program's by a relative error of at most 0.015.
Values may be sent and summed in bfloat16 or wider, within the bound.
No kernel may reach another device: no remote copies, remote signals or barrier semaphores. Data moves between devices by JAX's collectives and lax.ppermute only.
A program may use at most 128 MiB of HBM per device.

v0:
```python
import functools
import math

import jax
import jax.numpy as jnp
from jax import lax
from jax.experimental import pallas as pl
from jax.experimental.pallas import tpu as pltpu
from jax.sharding import PartitionSpec as P

D = 2048
HD = 128
BLK = 512
TILE = 128
STEPS = {"early": 4, "late": 12, "near": 12, "local": 3}


EPS = 1e-05
THETA = 10000.0
VMEM_LIMIT = 56 * 1024 * 1024
ATTEND_LIMIT = 32 * 1024 * 1024


def rotate(vectors, cosine, sine):
    half = vectors.shape[-1] // 2
    first = vectors[..., :half]
    second = vectors[..., half:]
    return jnp.concatenate(
        [first * cosine - second * sine, second * cosine + first * sine], axis=-1
    )


def general(hidden_in, norm_gain, w_qkv, w_out, block_lists):
    section_id = lax.axis_index("section")
    width = w_qkv.shape[2]
    heads_here = width // HD
    blocks_here = block_lists.shape[0]
    tok_dev = blocks_here * BLK
    scale = 1.0 / math.sqrt(HD)
    resid = hidden_in.astype(jnp.float32)
    normed = (
        resid * lax.rsqrt(jnp.mean(resid * resid, axis=-1, keepdims=True) + EPS) * norm_gain
    ).astype(jnp.bfloat16)
    flat_weight = w_qkv.reshape(D, 3 * width)
    frequency = THETA ** (-(2.0 * jnp.arange(HD // 2, dtype=jnp.float32)) / HD)
    piece = lax.all_gather(normed, "head", axis=0, tiled=True)
    count = piece.shape[0]
    mixed_rows = jnp.dot(piece, flat_weight, preferred_element_type=jnp.float32).reshape(
        count, 3, heads_here, HD
    )
    positions = (section_id * tok_dev + jnp.arange(count, dtype=jnp.int32)).astype(jnp.float32)
    angle = positions[:, None] * frequency[None, :]
    cosine = jnp.cos(angle)[:, None, :]
    sine = jnp.sin(angle)[:, None, :]
    query = rotate(mixed_rows[:, 0], cosine, sine).astype(jnp.bfloat16).reshape(count, width)
    keys = rotate(mixed_rows[:, 1], cosine, sine).astype(jnp.bfloat16).reshape(count, width)
    values = mixed_rows[:, 2].astype(jnp.bfloat16).reshape(count, width)
    keys_all, values_all = (
        lax.all_gather(keys, "section", axis=0, tiled=True),
        lax.all_gather(values, "section", axis=0, tiled=True),
    )
    count_blocks = block_lists.shape[0]
    query_blocks = query.reshape(count_blocks, BLK, heads_here, HD)
    block_ids = section_id * blocks_here + jnp.arange(count_blocks, dtype=jnp.int32)

    def one_block(carry, item):
        query_block, block_row, block_id = item
        live_slots = jnp.sum((block_row >= 0).astype(jnp.int32))
        query_positions = block_id * BLK + jnp.arange(BLK, dtype=jnp.int32)

        def one_slot(slot, state):
            highest, total, weighted = state
            source = block_row[slot]
            key_block = lax.dynamic_slice_in_dim(keys_all, source * BLK, BLK, 0).reshape(
                BLK, heads_here, HD
            )
            value_block = lax.dynamic_slice_in_dim(values_all, source * BLK, BLK, 0).reshape(
                BLK, heads_here, HD
            )
            scores = (
                jnp.einsum(
                    "qhd,khd->hqk", query_block, key_block, preferred_element_type=jnp.float32
                )
                * scale
            )
            key_positions = source * BLK + jnp.arange(BLK, dtype=jnp.int32)
            scores = jnp.where(
                key_positions[None, None, :] <= query_positions[None, :, None], scores, -jnp.inf
            )
            new_highest = jnp.maximum(highest, jnp.max(scores, axis=-1))
            factor = jnp.exp(highest - new_highest)
            weights = jnp.exp(scores - new_highest[..., None])
            total = total * factor + jnp.sum(weights, axis=-1)
            update = jnp.einsum(
                "hqk,khd->hqd",
                weights.astype(jnp.bfloat16),
                value_block,
                preferred_element_type=jnp.float32,
            )
            weighted = weighted * factor[..., None] + update
            return (new_highest, total, weighted)

        start_state = (
            jnp.full((heads_here, BLK), -jnp.inf, jnp.float32),
            jnp.zeros((heads_here, BLK), jnp.float32),
            jnp.zeros((heads_here, BLK, HD), jnp.float32),
        )
        highest, total, weighted = lax.fori_loop(0, live_slots, one_slot, start_state)
        result = (
            (weighted / total[..., None])
            .transpose(1, 0, 2)
            .reshape(BLK, width)
            .astype(jnp.bfloat16)
        )
        return (carry, result)

    _, results = lax.scan(
        one_block, jnp.zeros((), jnp.int32), (query_blocks, block_lists, block_ids)
    )
    attended = results.reshape(count_blocks * BLK, width)
    regrouped = lax.all_to_all(attended, "head", split_axis=0, concat_axis=1, tiled=True)
    summed = jnp.dot(
        regrouped,
        lax.all_gather(w_out, "head", axis=0, tiled=True),
        preferred_element_type=jnp.float32,
    )
    return (resid + summed).astype(jnp.bfloat16)


def project_kernel(number, noted, unrolled, halved, place, *rest):
    pieces, rest = rest[:number], rest[number:]
    if halved:
        beside, rest = rest[0], rest[1:]
    if noted:
        note, rest = rest[0], rest[1:]
    own, other, cosine, sine = rest[:4]
    outs, rest = rest[4:8], rest[8:]
    if halved:
        half = beside.shape[0] // 2
        (low, high), rest = rest[:2], rest[2:]
    rows, weights, results, row_sems, weight_sems, out_sems = rest[:6]
    count = rows.shape[0]
    half_copies, fetch_half = [], []
    if halved:
        staged = rest[6]
        fetch_half = [
            pltpu.make_async_copy(beside.at[pl.ds(half, half)], staged, row_sems.at[number])
        ]
        half_copies = [
            pltpu.make_async_copy(rows.at[pl.ds(0, half)], low, out_sems.at[4]),
            pltpu.make_async_copy(staged, high, out_sems.at[5]),
        ]
    row_copies, start = [], 0
    for i, ref in enumerate(pieces):
        size = ref.shape[0]
        row_copies.append(
            pltpu.make_async_copy(ref, rows.at[pl.ds(start, size)], row_sems.at[i])
        )
        start += size
    weight_copies = [
        pltpu.make_async_copy(
            ref.at[part],
            weights.at[w * 3 + part],
            weight_sems.at[w * 3 + part],
        )
        for w, ref in enumerate((own, other))
        for part in range(3)
    ]
    for copy in row_copies + weight_copies[:2] + fetch_half:
        copy.start()
    for copy in row_copies + fetch_half:
        copy.wait()
    for copy in half_copies:
        copy.start()
    query_scale = math.log2(math.e) / math.sqrt(HD)
    step = count // 2

    def out_copy(result, shift):
        return pltpu.make_async_copy(results.at[result], outs[shift], out_sems.at[shift])

    if noted:
        for result in range(4):
            results[result, count:, :] = note[...]

    for w in range(2):
        for part in range(3):
            weight_copies[w * 3 + part].wait()
            if w * 3 + part + 2 < 6:
                weight_copies[w * 3 + part + 2].start()

            def tile(i, carry, w=w, part=part):
                piece = pl.ds(pl.multiple_of(i * step, step), step)
                product = jnp.dot(
                    rows[piece], weights[w * 3 + part], preferred_element_type=jnp.float32
                )
                for h in range(2):
                    vector = product[:, h * HD : (h + 1) * HD]
                    if part < 2:
                        turned = pltpu.roll(vector, HD // 2, 1)
                        vector = vector * cosine[piece] + turned * sine[piece]
                    if part == 0:
                        vector = vector * query_scale
                    column = slice(part * HD, (part + 1) * HD)
                    results[w * 2 + h, piece, column] = vector.astype(jnp.bfloat16)
                return carry

            if unrolled:
                tile(0, 0)
                tile(1, 0)
            else:
                lax.fori_loop(0, 2, tile, 0)
        for h in range(2):
            for shift in range(4):

                @pl.when(place[shift] == w * 2 + h)
                def _(shift=shift, result=w * 2 + h):
                    out_copy(result, shift).start()

    for shift in range(4):
        out_copy(0, shift).wait()
    for copy in half_copies:
        copy.wait()


def project(place, pieces, own, other, cosine, sine, note, unrolled, beside):
    count = sum(piece.shape[0] for piece in pieces)
    number = len(pieces)
    width = own.shape[2]
    notes = [] if note is None else [note]
    extra = [] if beside is None else [beside]
    halves = [jax.ShapeDtypeStruct((count // 2, D), jnp.bfloat16)] * (2 * len(extra))
    full = count + sum(each.shape[0] for each in notes)
    any_space = pl.BlockSpec(memory_space=pl.ANY)
    vmem = pl.BlockSpec(memory_space=pltpu.VMEM)
    return pl.pallas_call(
        functools.partial(project_kernel, number, len(notes) > 0, unrolled, len(extra) > 0),
        out_shape=[jax.ShapeDtypeStruct((full, 3 * HD), jnp.bfloat16)] * 4 + halves,
        in_specs=[pl.BlockSpec(memory_space=pltpu.SMEM)]
        + [any_space] * (number + len(extra))
        + [vmem] * len(notes)
        + [any_space] * 2
        + [vmem] * 2,
        out_specs=[any_space] * (4 + len(halves)),
        scratch_shapes=[
            pltpu.VMEM((count, D), jnp.bfloat16),
            pltpu.VMEM((6, D, width), jnp.bfloat16),
            pltpu.VMEM((4, full, 3 * HD), jnp.bfloat16),
            pltpu.SemaphoreType.DMA((number + 1,)),
            pltpu.SemaphoreType.DMA((6,)),
            pltpu.SemaphoreType.DMA((6,)),
        ]
        + [pltpu.VMEM((count // 2, D), jnp.bfloat16)] * len(extra),
        compiler_params=pltpu.CompilerParams(vmem_limit_bytes=VMEM_LIMIT),
        cost_estimate=pl.CostEstimate(
            flops=2 * count * D * 6 * width, bytes_accessed=2 * 6 * D * width, transcendentals=0
        ),
        name="project_and_rotate",
    )(place, *pieces, *extra, *notes, own, other, cosine, sine)


def attend_kernel(mode, blocks_here, place, *refs):
    refs = list(refs)

    def take(number):
        taken = refs[:number]
        del refs[:number]
        return taken

    near, early, late = mode in ("near", "local"), mode == "early", mode == "late"
    steps = STEPS[mode]
    targets = {"near": (1, 2, 3), "local": (0,)}.get(mode, (0, 1, 2, 3))
    lists = take(4)
    have = (0, 2, 3) if early else (0, 1, 2, 3)
    here = {relative: take(4) for relative in have}
    there = {relative: take(4 if relative == 1 else 1) for relative in have}
    state = take(3) if late else []
    outs = take(3 if early else len(targets))
    if early:
        queries, tops, sums = outs
        rows, query_rows, values_t, item_q, item_k, table, sems = refs
    else:
        rows, query_rows, values_t, queries, tops, sums, item_q, item_k, table, sems = refs
    section, chip, core = place[0], place[1], place[2]
    rows_here = here[2][0].shape[0]
    tok = blocks_here * BLK
    slots = lists[0].shape[1]
    wide = 2 * TILE
    pair_blocks = blocks_here // 2
    total_blocks = 4 * pair_blocks
    own_pair = chip // 2
    pair = own_pair if near else 1 - own_pair
    parity = lax.rem(chip, 2)

    def fetches(relatives, with_queries, first):
        copies = []
        for shift in range(4):
            number, query_number = first + shift * 12, first + shift * 12 + 8
            for relative in relatives:
                owner = chip ^ relative
                source = lax.rem(section - shift + 4, 4)
                for far in range(2):
                    side = core if far == 0 else 1 - core
                    if far == 0:
                        ref = here[relative][shift]
                    elif relative == 1:
                        ref = there[relative][shift]
                    else:
                        ref = there[relative][0].at[shift]
                    start = source * tok + owner * (2 * rows_here) + side * rows_here
                    start = pl.multiple_of(start, rows_here)
                    copies.append(
                        pltpu.make_async_copy(
                            ref.at[pl.ds(0, rows_here), pl.ds(HD, 2 * HD)],
                            rows.at[pl.ds(start, rows_here)],
                            sems.at[number],
                        )
                    )
                    number += 1
                    if not with_queries or (relative < 2) != near:
                        continue
                    start = source * (tok // 2) + lax.rem(owner, 2) * (2 * rows_here)
                    start = pl.multiple_of(start + side * rows_here, rows_here)
                    copies.append(
                        pltpu.make_async_copy(
                            ref.at[pl.ds(0, rows_here), pl.ds(0, HD)],
                            query_rows.at[pl.ds(start, rows_here)],
                            sems.at[query_number],
                        )
                    )
                    query_number += 1
        return copies

    def key_block(block):
        return block // pair_blocks * blocks_here + pair * pair_blocks + lax.rem(block, pair_blocks)

    copies = fetches((0, 1) if late else have, not late, 0)
    state_copies = [
        pltpu.make_async_copy(ref, held, sems.at[48 + i])
        for i, (ref, held) in enumerate(zip(state, (queries, tops, sums)))
    ]
    for copy in copies + state_copies:
        copy.start()

    count = jnp.int32(0)
    for target in targets:
        block_list = lists[(4 - target) % 4]
        first_block = lax.rem(section + target, 4) * pair_blocks

        def note(local, count, block_list=block_list, first_block=first_block):
            def one(slot, count, local=local):
                source = block_list[pair * pair_blocks + local, slot]
                item_q[count] = first_block + local
                item_k[count] = source
                table[(first_block + local) * slots + slot] = source
                wanted = source >= 0
                if not near:
                    in_section = lax.rem(jnp.maximum(source, 0), blocks_here)
                    whole = (in_section // pair_blocks != own_pair) | (
                        lax.rem(in_section, pair_blocks) == parity * (pair_blocks - 1)
                    )
                    wanted = wanted & (whole if early else jnp.logical_not(whole))
                return count + wanted.astype(jnp.int32)

            if mode in ("early", "local"):
                return lax.fori_loop(1, slots, one, count)
            for slot in range(1, slots):
                count = one(slot, count)
            return count

        count = lax.fori_loop(0, pair_blocks, note, count)
    for extra in range(steps):
        item_q[count + extra] = total_blocks
        item_k[count + extra] = (own_pair if late else pair) * pair_blocks

    values_t[HD:, :] = jnp.ones((values_t.shape[0] - HD, values_t.shape[1]), jnp.bfloat16)
    if not late:
        queries[total_blocks] = jnp.zeros((wide, HD), jnp.bfloat16)
        tops[total_blocks] = jnp.zeros((8, wide), jnp.float32)
        sums[total_blocks] = jnp.zeros(sums.shape[1:], jnp.float32)

    lane = lax.broadcasted_iota(jnp.int32, (BLK, wide), 1)
    key_at = lax.broadcasted_iota(jnp.int32, (BLK, wide), 0)

    def query_place(local):
        middle = local == 1
        return jnp.where(middle, core * TILE, core * wide), jnp.where(middle, TILE, 0)

    def scores_of(source, query):
        at = pl.multiple_of(source * BLK, BLK)
        return lax.dot_general(
            rows[pl.ds(at, BLK), 0:HD],
            query,
            (((1,), (1,)), ((), ())),
            preferred_element_type=jnp.float32,
        )

    def weigh(source, weights):
        at = pl.multiple_of(source * BLK, BLK)
        return jnp.dot(
            values_t[:, pl.ds(at, BLK)],
            weights.astype(jnp.bfloat16),
            preferred_element_type=jnp.float32,
        )

    def masked(local, scores):
        offset, gap = query_place(local)
        query_at = offset + lane + jnp.where(lane >= TILE, gap, 0)
        return jnp.where(key_at <= query_at, scores, -jnp.inf)

    def diagonal(first):
        blocks = [first + local for local in range(pair_blocks)]
        scores = []
        for local, block in enumerate(blocks):
            offset, gap = query_place(local)
            start = pl.multiple_of(block * BLK + offset, TILE)
            later = pl.multiple_of(start + TILE + gap, TILE)
            query = jnp.concatenate(
                [query_rows[pl.ds(start, TILE)], query_rows[pl.ds(later, TILE)]], axis=0
            )
            queries[block] = query
            scores.append(scores_of(key_block(block), query))
        for local, (block, score) in enumerate(zip(blocks, scores)):
            score = masked(local, score)
            top = jnp.max(score, axis=0, keepdims=True)
            tops[block] = jnp.broadcast_to(top, (8, wide))
            sums[block] = weigh(key_block(block), jnp.exp2(score - top))

    def turn(first, number):
        for i in range(number):
            at = pl.multiple_of((first + i) * BLK, BLK)
            values_t[:HD, pl.ds(at, BLK)] = rows[pl.ds(at, BLK), HD : 2 * HD].T

    waits = 4 if late else 2 * len(have)

    def arrive(shift, carry):
        source = lax.rem(section - shift + 4, 4)
        for number in range(waits):
            pltpu.make_async_copy(
                rows.at[pl.ds(0, rows_here)],
                rows.at[pl.ds(0, rows_here)],
                sems.at[shift * 12 + number],
            ).wait()
        if late:
            turn(source * blocks_here + own_pair * pair_blocks, pair_blocks)
            return carry
        for number in range(4):
            pltpu.make_async_copy(
                query_rows.at[pl.ds(0, rows_here)],
                query_rows.at[pl.ds(0, rows_here)],
                sems.at[shift * 12 + 8 + number],
            ).wait()
        turn(source * blocks_here, blocks_here)
        if mode == "early":
            diagonal(source * pair_blocks)
        else:
            wanted = shift == 0 if mode == "local" else shift != 0
            pl.when(wanted)(lambda: diagonal(source * pair_blocks))
        return carry

    lax.fori_loop(0, 4, arrive, 0)
    for copy in state_copies:
        copy.wait()

    def below(step, carry):
        items = [step * steps + i for i in range(steps)]
        scores = scores_of(item_k[items[0]], queries[item_q[items[0]]])
        held = None
        for i, item in enumerate(items):
            if i + 1 < steps:
                ahead = scores_of(item_k[items[i + 1]], queries[item_q[items[i + 1]]])
            weights = jnp.exp2(scores - tops[item_q[item], 0:1]).astype(jnp.bfloat16)
            if held is not None:
                sums[item_q[items[i - 1]]] += weigh(item_k[items[i - 1]], held)
            held, scores = weights, ahead
        sums[item_q[items[-1]]] += weigh(item_k[items[-1]], held)
        return carry

    lax.fori_loop(0, (count + steps - 1) // steps, below, 0)
    if early:
        return

    def over_in(i, over):
        block = lax.rem(section * pair_blocks + targets[0] * pair_blocks + i, total_blocks)
        return jnp.maximum(over, jnp.where(sums[block, HD : HD + 1] < 2.0**100, 0.0, 1.0))

    number_blocks = len(targets) * pair_blocks
    over = lax.fori_loop(0, number_blocks, over_in, jnp.zeros((1, wide), jnp.float32))

    @pl.when(jnp.max(over) > 0)
    def _():
        if late:
            copies = fetches((2, 3), False, 0)
            for copy in copies:
                copy.start()
            for copy in copies:
                copy.wait()

            def turn_all(step, carry):
                turn(step * pair_blocks, pair_blocks)
                return carry

            lax.fori_loop(0, 8, turn_all, 0)

        def one_block(i, carry):
            block = lax.rem(section * pair_blocks + targets[0] * pair_blocks + i, total_blocks)
            home = key_block(block)
            query = queries[block]
            scores = masked(lax.rem(block, pair_blocks), scores_of(home, query))
            highest = jnp.max(scores, axis=0, keepdims=True)
            weighted = weigh(home, jnp.exp2(scores - highest))

            def one_slot(slot, state):
                highest, weighted = state
                source = table[block * slots + slot]
                scores = scores_of(jnp.maximum(source, 0), query)
                scores = jnp.where(source >= 0, scores, -jnp.inf)
                new_highest = jnp.maximum(highest, jnp.max(scores, axis=0, keepdims=True))
                weights = jnp.exp2(scores - new_highest)
                weighted = weighted * jnp.exp2(highest - new_highest)
                weighted = weighted + weigh(jnp.maximum(source, 0), weights)
                return (new_highest, weighted)

            _, sums[block] = lax.fori_loop(1, slots, one_slot, (highest, weighted))
            return carry

        lax.fori_loop(0, number_blocks, one_block, 0)

    for number, target in enumerate(targets):

        def leave(local, carry, number=number, target=target):
            block = lax.rem(section + target, 4) * pair_blocks + local
            result = (sums[block, 0:HD] / sums[block, HD : HD + 1]).T.astype(jnp.bfloat16)
            for part in range(2):
                tile = 2 * local + part
                upper = (tile >= 3).astype(jnp.int32)
                i = tile - 3 * upper
                which = upper ^ parity
                given = i == 2 - 2 * core
                if near:
                    where = jnp.where(given, 4 + which, which * 2 + i - core)
                else:
                    where = which * 3 + jnp.where(given, 2, i - core)
                outs[number][where] = result[part * TILE : (part + 1) * TILE]
            return carry

        lax.fori_loop(0, pair_blocks, leave, 0)


def attend(mode, place, lists, here, there, state=()):
    blocks_here, slots = lists[0].shape
    total_blocks = 2 * blocks_here
    tokens = 4 * blocks_here * BLK
    room = total_blocks * slots + STEPS[mode]
    pairs = total_blocks * slots // 4
    have = (0, 2, 3) if mode == "early" else (0, 1, 2, 3)
    pieces = [piece for relative in have for piece in here[relative]]
    pieces += [piece for relative in have for piece in there[relative]]
    sums = [
        jax.ShapeDtypeStruct((total_blocks + 1, 2 * TILE, HD), jnp.bfloat16),
        jax.ShapeDtypeStruct((total_blocks + 1, 8, 2 * TILE), jnp.float32),
        jax.ShapeDtypeStruct((total_blocks + 1, HD + 16, 2 * TILE), jnp.float32),
    ]
    if mode == "early":
        outs = sums
    else:
        number = {"late": 4, "near": 3, "local": 1}[mode]
        outs = [jax.ShapeDtypeStruct((blocks_here, TILE, HD), jnp.bfloat16)] * number
    held = [] if mode == "early" else [pltpu.VMEM(each.shape, each.dtype) for each in sums]
    return pl.pallas_call(
        functools.partial(attend_kernel, mode, blocks_here),
        out_shape=outs,
        in_specs=[pl.BlockSpec(memory_space=pltpu.SMEM)] * 5
        + [pl.BlockSpec(memory_space=pl.ANY)] * (len(pieces) + len(state)),
        out_specs=[pl.BlockSpec(memory_space=pltpu.VMEM)] * len(outs),
        scratch_shapes=[
            pltpu.VMEM((tokens, 2 * HD), jnp.bfloat16),
            pltpu.VMEM((tokens // 2, HD), jnp.bfloat16),
            pltpu.VMEM((HD + 16, tokens), jnp.bfloat16),
            *held,
            pltpu.SMEM((room,), jnp.int32),
            pltpu.SMEM((room,), jnp.int32),
            pltpu.SMEM((room,), jnp.int32),
            pltpu.SemaphoreType.DMA((51,)),
        ],
        compiler_params=pltpu.CompilerParams(vmem_limit_bytes=ATTEND_LIMIT),
        cost_estimate=pl.CostEstimate(
            flops=pairs * 4 * BLK * 2 * TILE * HD,
            bytes_accessed=tokens * 5 * HD,
            transcendentals=pairs * BLK * 2 * TILE,
        ),
        name="attend_" + mode,
    )(place, *lists, *pieces, *state)


def finish_kernel(relatives, kept_parts, place, *rest):
    number = len(relatives)
    kept = []
    for parts in kept_parts:
        kept.append(rest[:parts])
        rest = rest[parts:]
    given, rest = rest[:number], rest[number:]
    w_out, hidden, out, attended, weights, sums, sems, given_sems, weight_sems = rest
    section, chip, core = place[0], place[1], place[2]
    odd = lax.rem(chip, 2)
    depth = 4 * HD
    copies = []
    for r, relative in enumerate(relatives):
        start = pl.multiple_of((chip ^ relative) * depth, depth)
        group = [
            pltpu.make_async_copy(w_out.at[pl.ds(start, depth)], weights.at[r], weight_sems.at[r])
        ]
        for shift in range(4):
            head = lax.rem(section - shift + 4, 4)
            column = pl.ds(pl.multiple_of(head * HD, HD), HD)
            for slot in range(2):
                to = jnp.where(core == 0, slot * (1 + odd), odd if slot == 0 else 2)
                source = kept[r][0].at[shift] if kept_parts[r] == 1 else kept[r][shift]
                group.append(
                    pltpu.make_async_copy(
                        source.at[slot],
                        attended.at[r, pl.ds(pl.multiple_of(to * TILE, TILE), TILE), column],
                        sems.at[(r * 4 + shift) * 2 + slot],
                    )
                )
            to = jnp.where(core == 0, 2 - odd, 1 - odd)
            group.append(
                pltpu.make_async_copy(
                    given[r].at[shift, 0],
                    attended.at[r, pl.ds(pl.multiple_of(to * TILE, TILE), TILE), column],
                    given_sems.at[r * 4 + shift],
                )
            )
        copies.append(group)
    for copy in copies[0] + copies[1]:
        copy.start()
    half = out.shape[0] // 2
    step = 512
    for r in range(number):
        for copy in copies[r]:
            copy.wait()
        if r + 2 < number:
            for copy in copies[r + 2]:
                copy.start()

        def columns(i, carry, r=r):
            column = pl.ds(pl.multiple_of(i * step, step), step)
            for at in range(0, out.shape[0], half):
                piece = (slice(at, at + half), column)
                summed = jnp.dot(
                    attended[r, at : at + half],
                    weights[r, :, column],
                    preferred_element_type=jnp.float32,
                )
                summed = summed + (hidden[piece].astype(jnp.float32) if r == 0 else sums[piece])
                if r + 1 < number:
                    sums[piece] = summed
                else:
                    out[piece] = summed.astype(out.dtype)
            return carry

        for i in range(out.shape[1] // step):
            columns(i, 0)


def finish(relatives, place, kept, given, w_out, hidden):
    count = hidden.shape[0]
    number = len(relatives)
    any_space = pl.BlockSpec(memory_space=pl.ANY)
    vmem = pl.BlockSpec(memory_space=pltpu.VMEM)
    depth = 4 * HD
    return pl.pallas_call(
        functools.partial(finish_kernel, relatives, [len(parts) for parts in kept]),
        out_shape=jax.ShapeDtypeStruct((count, D), jnp.bfloat16),
        in_specs=[pl.BlockSpec(memory_space=pltpu.SMEM)]
        + [any_space] * (sum(map(len, kept)) + number + 1)
        + [vmem],
        out_specs=vmem,
        scratch_shapes=[
            pltpu.VMEM((number, count, depth), jnp.bfloat16),
            pltpu.VMEM((number, depth, D), jnp.bfloat16),
            pltpu.VMEM((count, D), jnp.float32),
            pltpu.SemaphoreType.DMA((number * 8,)),
            pltpu.SemaphoreType.DMA((number * 4,)),
            pltpu.SemaphoreType.DMA((number,)),
        ],
        compiler_params=pltpu.CompilerParams(vmem_limit_bytes=VMEM_LIMIT),
        cost_estimate=pl.CostEstimate(
            flops=2 * count * D * D, bytes_accessed=2 * D * D, transcendentals=0
        ),
        name="project_out",
    )(place, *[part for parts in kept for part in parts], *given, w_out, hidden)


def by_head(hidden_in, norm_gain, w_qkv, w_out, block_lists):
    section = lax.axis_index("section")
    device = lax.axis_index("head")
    chip, core = device // 2, device % 2
    blocks_here = block_lists.shape[0]
    tok = blocks_here * BLK
    rows = hidden_in.shape[0]
    half = rows // 2

    other_core = [(i, i ^ 1) for i in range(8)]
    along_x = [(i, i ^ 2) for i in range(8)]
    along_y = [(i, i ^ 4) for i in range(8)]

    def to_section(array, shift):
        return lax.ppermute(array, "section", [(i, (i + shift) % 4) for i in range(4)])

    place = jnp.stack([section, chip, core]).astype(jnp.int32)
    shifts = jnp.arange(4, dtype=jnp.int32)
    chosen = (section + shifts - 2 * core + 4) % 4

    own = jnp.transpose(w_qkv, (1, 0, 2))
    other = lax.ppermute(own, "head", other_core)
    hidden_in, own = lax.optimization_barrier((hidden_in, own))

    resid = hidden_in.astype(jnp.float32)
    normed = (
        resid * lax.rsqrt(jnp.mean(resid * resid, axis=-1, keepdims=True) + EPS) * norm_gain
    ).astype(jnp.bfloat16)
    y_rows = lax.ppermute(normed, "head", along_y)
    x_rows = lax.ppermute(normed, "head", along_x)

    frequency = THETA ** (-(2.0 * jnp.arange(HD // 2, dtype=jnp.float32)) / HD)

    def projected(relatives, pieces, note=None, unrolled=False, beside=None, base=None):
        starts = (section if base is None else base) * tok + (chip ^ jnp.array(relatives)) * (2 * rows) + core * rows
        positions = (starts[:, None] + jnp.arange(rows, dtype=jnp.int32)[None, :]).reshape(-1)
        angle = positions.astype(jnp.float32)[:, None] * frequency
        cosine, sine = jnp.cos(angle), jnp.sin(angle)
        cosine = jnp.concatenate([cosine, cosine], axis=-1)
        sine = jnp.concatenate([-sine, sine], axis=-1)
        return project(chosen, pieces, own, other, cosine, sine, note, unrolled, beside)

    def sent(outs):
        return [outs[0]] + [to_section(outs[shift], shift) for shift in range(1, 4)]

    def to_other(array):
        return lax.ppermute(array, "head", other_core)

    def after(first, second):
        joined = lax.optimization_barrier((*first, *second))
        return list(joined[: len(first)]), list(joined[len(first) :])

    note = jnp.pad(
        block_lists.astype(jnp.bfloat16),
        ((0, 16 - blocks_here), (0, 3 * HD - block_lists.shape[1])),
    )
    own_outs = projected([0], [normed], note, True)
    own_outs, (base,) = after(own_outs, [section])
    own_parts = sent(own_outs)
    *y_outs, y_low, x_high = projected([2], [y_rows], None, True, x_rows, base)
    own_parts, held = after(own_parts, [x_high, y_low, *y_outs])
    x_high, y_low, *y_outs = held
    d_low = lax.ppermute(y_low, "head", along_x)
    d_high = lax.ppermute(x_high, "head", along_y)
    y_parts = sent(y_outs)
    d_outs = projected([3], [d_low, d_high], base=base)
    y_parts, held = after(y_parts, [w_out, x_rows, *d_outs])
    w_out, x_rows, *d_outs = held
    lists = [block_lists] + [
        part[rows : rows + blocks_here, : block_lists.shape[1]].astype(jnp.int32)
        for part in own_parts[1:]
    ]
    w_out_all = lax.all_gather(w_out, "head", axis=0, tiled=True)
    d_parts = sent(d_outs)
    d_parts, x_outs = after(d_parts, projected([1], [x_rows], base=base))
    x_parts = sent(x_outs)

    here = {0: own_parts, 1: x_parts, 2: y_parts, 3: d_parts}
    there = {relative: [to_other(jnp.stack(here[relative]))] for relative in (0, 2, 3)}
    state = attend("early", place, lists, here, there)
    x_parts, state = after(x_parts, state)
    here[1], there[1] = x_parts, [to_other(part) for part in x_parts]

    def to_chip(array, relative, cross):
        flip = 2 * relative + (1 if cross else 0)
        return lax.ppermute(array, "head", [(i, i ^ flip) for i in range(8)])

    far = attend("late", place, lists, here, there, state)
    far = [far[0]] + [to_section(far[shift], shift) for shift in range(1, 4)]
    near = attend("near", place, lists, here, there)
    near, (place, *far) = after(near, [place, *far])
    y_part = to_chip(jnp.stack([part[0:3] for part in far]), 2, False)
    d_part = to_chip(jnp.stack([part[3:6] for part in far]), 3, False)
    near = [to_section(near[shift - 1], shift) for shift in range(1, 4)]
    near = [*attend("local", place, lists, here, there), *near]
    swapped = to_other(jnp.stack([y_part[:, 2:3], d_part[:, 2:3]]))
    x_kept = to_chip(jnp.stack([part[2:4] for part in near]), 1, False)
    x_given = to_chip(jnp.stack([part[5:6] for part in near]), 1, True)
    own_given = to_other(jnp.stack([part[4:5] for part in near]))
    kept = [near, [x_kept], [y_part], [d_part]]
    given = [own_given, x_given, swapped[0], swapped[1]]
    return finish((0, 1, 2, 3), place, kept, given, w_out_all, hidden_in)


def solution(mesh):
    placed = (
        P(("section", "head"), None),
        P(),
        P(None, None, "head"),
        P("head", None),
        P("section", None),
    )

    def local(hidden_in, norm_gain, w_qkv, w_out, block_lists):
        fits = (
            mesh.shape["section"] == 4
            and mesh.shape["head"] == 8
            and w_qkv.shape[2] == 2 * HD
            and block_lists.shape[0] == 6
            and hidden_in.shape[0] == 3 * TILE
        )
        form = by_head if fits else general
        return form(hidden_in, norm_gain, w_qkv, w_out, block_lists)

    return jax.shard_map(
        local, mesh=mesh, in_specs=placed, out_specs=P(("section", "head"), None), check_vma=False
    )
```

profile of v0, /device:TPU:0, one launch (start us, length us, event | category | flops | bytes accessed | tf_op | source)
XLA Modules:
  0.0 230.1 jit_solution(14273103883094407158)
XLA Ops:
  7.0 1.8 fusion
  8.9 1.6 fusion.2.rest_0_
  10.4 2.6 %collective-permute-start.5 = (bf16[384,2048]{1,0:T(8,128)(2,1)}, bf16[384,2048]{1,0:T(8,128)(2,1)S(1)}, u32[]{:S(2)}, u32[]{:S(2)}) collective-permute-start(bf16[384,2048]{1,0:T(8,128)(2,1)} %fusion.2.rest_0_), channel_id=1, source_target_pairs={{0,2},{1,3},{2,0},{3,1},{4,6},{5,7},{6,4},{7,5},{8,10},{9,11},{10,... | collective-permute-start | bytes 4718600 | tf_op jit(solution)/shard_map/ppermute | solution.py:723
  13.0 1.5 collective-permute-start.4
  16.5 0.9 pad_maximum_fusion.7
  17.5 7.8 %project_and_rotate.4 = (bf16[400,384]{1,0:T(8,128)(2,1)}, bf16[400,384]{1,0:T(8,128)(2,1)}, bf16[400,384]{1,0:T(8,128)(2,1)}, bf16[400,384]{1,0:T(8,128)(2,1)}) custom-call(s32[4]{0:T(128)} %and_select_fusion.place, bf16[384,2048]{1,0:T(8,128)(2,1)} %fusion.2.rest_0_, bf16[16,384]{1,0:T(8,128)(2,1)} %pad.4.rest_1_, bf16[3,2048,256]{2,1,0:T(8,128)(2,1)} %bitcast.90, ...), custom_call_target="tpu_custom_call" | custom-call | flops 2415919104 | bytes 6291456 | tf_op jit(solution)/shard_map/project_and_rotate/pallas_call | solution.py:235
  25.3 1.6 collective-permute-start.1
  27.0 2.6 %collective-permute-start.2 = (bf16[400,384]{1,0:T(8,128)(2,1)}, bf16[400,384]{1,0:T(8,128)(2,1)S(1)}, u32[]{:S(2)}, u32[]{:S(2)}) collective-permute-start(bf16[400,384]{1,0:T(8,128)(2,1)} %get-tuple-element.91), channel_id=1, source_target_pairs={{0,16},{8,24},{16,0},{24,8},{1,17},{9,25},{17,1},{25,9},{2,18},{10... | collective-permute-start | bytes 921608 | tf_op jit(solution)/shard_map/ppermute | solution.py:708
  29.6 1.4 collective-permute-start.3
  30.9 2.1 fusion.6
  34.7 13.5 %collective-permute-done.5.rest_1_.rest_0_ = bf16[384,2048]{1,0:T(8,128)(2,1)S(1)} collective-permute-done((bf16[384,2048]{1,0:T(8,128)(2,1)}, bf16[384,2048]{1,0:T(8,128)(2,1)S(1)}, u32[]{:S(2)}, u32[]{:S(2)}) %collective-permute-start.5) | collective-permute-done | bytes 1572896 | tf_op jit(solution)/shard_map/ppermute | solution.py:723
  48.2 1.6 collective-permute-done.4.rest_0_
  49.7 8.7 %project_and_rotate.5 = (bf16[384,384]{1,0:T(8,128)(2,1)}, bf16[384,384]{1,0:T(8,128)(2,1)}, bf16[384,384]{1,0:T(8,128)(2,1)}, bf16[384,384]{1,0:T(8,128)(2,1)},...) custom-call(s32[4]{0:T(128)} %and_select_fusion.place, bf16[384,2048]{1,0:T(8,128)(2,1)} %collective-permute-done.4.rest_0_, ...), custom_call_target="tpu_custom_call" | custom-call | flops 2415919104 | bytes 6291456 | tf_op jit(solution)/shard_map/project_and_rotate/pallas_call | solution.py:235
  58.5 1.6 collective-permute-start.10
  60.1 1.3 collective-permute-start.9
  62.2 1.6 collective-permute-start.6
  63.8 2.6 %collective-permute-start.7 = (bf16[384,384]{1,0:T(8,128)(2,1)}, bf16[384,384]{1,0:T(8,128)(2,1)S(1)}, u32[]{:S(2)}, u32[]{:S(2)}) collective-permute-start(bf16[384,384]{1,0:T(8,128)(2,1)} %get-tuple-element.106), channel_id=1, source_target_pairs={{0,16},{8,24},{16,0},{24,8},{1,17},{9,25},{17,1},{25,9},{2,18},{10... | collective-permute-start | bytes 884744 | tf_op jit(solution)/shard_map/ppermute | solution.py:708
  66.4 1.3 collective-permute-start.8
  68.6 9.2 %collective-permute-done.10.rest_1_ = bf16[192,2048]{1,0:T(8,128)(2,1)S(1)} collective-permute-done((bf16[192,2048]{1,0:T(8,128)(2,1)}, bf16[192,2048]{1,0:T(8,128)(2,1)S(1)}, u32[]{:S(2)}, u32[]{:S(2)}) %collective-permute-start.10) | collective-permute-done | bytes 786464 | tf_op jit(solution)/shard_map/ppermute | solution.py:757
  77.8 1.2 collective-permute-done.9.rest_0_
  79.0 0.9 copy-done.18
  79.9 9.0 %project_and_rotate.6 = (bf16[384,384]{1,0:T(8,128)(2,1)}, bf16[384,384]{1,0:T(8,128)(2,1)}, bf16[384,384]{1,0:T(8,128)(2,1)}, bf16[384,384]{1,0:T(8,128)(2,1)}) custom-call(s32[4]{0:T(128)} %and_select_fusion.place, bf16[192,2048]{1,0:T(8,128)(2,1)} %copy-done.18, bf16[192,2048]{1,0:T(8,128)(2,1)} %copy-done.17, bf16[3,2048,256]{2,1,0:T(8,128)(2,1)} %bitcast.92, ...), custom_call_target="tpu_custom_call" | custom-call | flops 2415919104 | bytes 6291456 | tf_op jit(solution)/shard_map/project_and_rotate/pallas_call | solution.py:235
  91.5 3.0 %collective-permute-start.11 = (bf16[384,384]{1,0:T(8,128)(2,1)S(1)}, bf16[384,384]{1,0:T(8,128)(2,1)S(1)}, u32[]{:S(2)}, u32[]{:S(2)}) collective-permute-start(bf16[384,384]{1,0:T(8,128)(2,1)S(1)} %copy-done.22), channel_id=1, source_target_pairs={{0,8},{8,16},{16,24},{24,0},{1,9},{9,17},{17,25},{25,1},{2,10},{10... | collective-permute-start | bytes 884744 | tf_op jit(solution)/shard_map/ppermute | solution.py:708
  94.5 1.6 collective-permute-start.12
  96.1 0.9 collective-permute-start.13
  96.9 1.2 pad_maximum_fusion.1
  98.1 9.1 %project_and_rotate.7 = (bf16[384,384]{1,0:T(8,128)(2,1)}, bf16[384,384]{1,0:T(8,128)(2,1)}, bf16[384,384]{1,0:T(8,128)(2,1)}, bf16[384,384]{1,0:T(8,128)(2,1)}) custom-call(s32[4]{0:T(128)} %and_select_fusion.place, bf16[384,2048]{1,0:T(8,128)(2,1)} %copy-done.8, bf16[3,2048,256]{2,1,0:T(8,128)(2,1)} %bitcast.93, ...), custom_call_target="tpu_custom_call" | custom-call | flops 2415919104 | bytes 6291456 | tf_op jit(solution)/shard_map/project_and_rotate/pallas_call | solution.py:235
  107.2 8.0 %collective-permute-done.12.refs_14_.refs_18_ = bf16[384,384]{1,0:T(8,128)(2,1)S(1)} collective-permute-done((bf16[384,384]{1,0:T(8,128)(2,1)S(1)}, bf16[384,384]{1,0:T(8,128)(2,1)S(1)}, u32[]{:S(2)}, u32[]{:S(2)}) %collective-permute-start.12) | collective-permute-done | bytes 294944 | tf_op jit(solution)/shard_map/ppermute | solution.py:708
  115.6 7.0 %collective-permute-start.14 = (bf16[384,384]{1,0:T(8,128)(2,1)S(1)}, bf16[384,384]{1,0:T(8,128)(2,1)S(1)}, u32[]{:S(2)}, u32[]{:S(2)}) collective-permute-start(bf16[384,384]{1,0:T(8,128)(2,1)S(1)} %copy-done.24), channel_id=1, source_target_pairs={{0,8},{8,16},{16,24},{24,0},{1,9},{9,17},{17,25},{25,1},{2,10},{10... | collective-permute-start | bytes 884744 | tf_op jit(solution)/shard_map/ppermute | solution.py:708
  122.6 1.4 collective-permute-start.15
  124.0 1.1 collective-permute-start.16
  125.1 17.5 %attend_early.1 = (bf16[13,256,128]{2,1,0:T(8,128)(2,1)S(1)}, f32[13,8,256]{2,1,0:T(8,128)S(1)}, f32[13,144,256]{2,1,0:T(8,128)S(1)}) custom-call(s32[3]{0:T(128)S(1)} %pad_add_fusion.place, s32[6,12]{1,0:T(8,128)S(1)} %copy-done.5, s32[6,12]{1,0:T(8,128)S(1)} %slice_convert_fusion.2.refs_1_, s32[6,12]{1,0:T(8,128)S(1)} %slice_convert_fusion.1.refs_2_, ...), custom_call_target="tpu_custom_call" | custom-call | flops 2415919104 | bytes 7864320 | tf_op jit(solution)/shard_map/attend_early/pallas_call | solution.py:569
  142.6 1.2 collective-permute-done.15.refs_10_
  146.7 11.2 %attend_late.1 = (bf16[6,128,128]{2,1,0:T(8,128)(2,1)S(1)}, bf16[6,128,128]{2,1,0:T(8,128)(2,1)S(1)}, bf16[6,128,128]{2,1,0:T(8,128)(2,1)S(1)}, bf16[6,128,128]{2,1,0:T(8,128)(2,1)S(1)}) custom-call(s32[3]{0:T(128)S(1)} %pad_add_fusion.place, s32[6,12]{1,0:T(8,128)S(1)} %copy-done.5, s32[6,12]{1,0:T(8,128)S(1)} %slice_convert_fusion.2.refs_1_, ...), custom_call_target="tpu_custom_call" | custom-call | flops 2415919104 | bytes 7864320 | tf_op jit(solution)/shard_map/attend_late/pallas_call | solution.py:569
  157.9 6.9 %collective-permute-start.24 = (bf16[6,128,128]{2,1,0:T(8,128)(2,1)S(1)}, bf16[6,128,128]{2,1,0:T(8,128)(2,1)S(1)}, u32[]{:S(2)}, u32[]{:S(2)}) collective-permute-start(bf16[6,128,128]{2,1,0:T(8,128)(2,1)S(1)} %get-tuple-element.149), channel_id=1, source_target_pairs={{0,8},{8,16},{16,24},{24,0},{1,9},{9,17},{17,25},{25,1},{2,10},{10... | collective-permute-start | bytes 589832 | tf_op jit(solution)/shard_map/ppermute | solution.py:708
  164.7 1.4 collective-permute-start.25
  166.1 1.1 collective-permute-start.26
  167.2 15.5 %attend_near.1 = (bf16[6,128,128]{2,1,0:T(8,128)(2,1)S(1)}, bf16[6,128,128]{2,1,0:T(8,128)(2,1)S(1)}, bf16[6,128,128]{2,1,0:T(8,128)(2,1)S(1)}) custom-call(s32[3]{0:T(128)S(1)} %pad_add_fusion.place, s32[6,12]{1,0:T(8,128)S(1)} %copy-done.5, s32[6,12]{1,0:T(8,128)S(1)} %slice_convert_fusion.2.refs_1_, s32[6,12]{1,0:T(8,128)S(1)} %slice_convert_fusion.1.refs_2_, ...), custom_call_target="tpu_custom_call" | custom-call | flops 2415919104 | bytes 7864320 | tf_op jit(solution)/shard_map/attend_near/pallas_call | solution.py:569
  182.9 1.8 collective-permute-start.32
  185.7 1.2 collective-permute-start.27
  186.8 1.6 collective-permute-start.28
  188.4 1.1 collective-permute-start.29
  189.5 5.4 %attend_local.1.rest_0_ = bf16[6,128,128]{2,1,0:T(8,128)(2,1)S(1)} custom-call(s32[3]{0:T(128)S(1)} %pad_add_fusion.place, s32[6,12]{1,0:T(8,128)S(1)} %copy-done.5, s32[6,12]{1,0:T(8,128)S(1)} %slice_convert_fusion.2.refs_1_, s32[6,12]{1,0:T(8,128)S(1)} %slice_convert_fusion.1.refs_2_, s32[6,12]{1,0:T(8,128)S(1)} %slice_convert_fusion.refs_3_, ...), custom_call_target="tpu_custom_call" | custom-call | flops 2415919104 | bytes 7864320 | tf_op jit(solution)/shard_map/attend_local/pallas_call | solution.py:569
  195.5 6.4 %collective-permute-done.28.rest_2_ = bf16[6,128,128]{2,1,0:T(8,128)(2,1)S(1)} collective-permute-done((bf16[6,128,128]{2,1,0:T(8,128)(2,1)S(1)}, bf16[6,128,128]{2,1,0:T(8,128)(2,1)S(1)}, u32[]{:S(2)}, u32[]{:S(2)}) %collective-permute-start.28) | collective-permute-done | bytes 196640 | tf_op jit(solution)/shard_map/ppermute | solution.py:708
  203.3 1.2 collective-permute-start.30
  206.1 1.6 collective-permute-done.34.rest_8_
  207.7 5.7 %collective-permute-done.30.rest_4_ = bf16[4,2,128,128]{3,2,1,0:T(8,128)(2,1)S(1)} collective-permute-done((bf16[4,2,128,128]{3,2,1,0:T(8,128)(2,1)S(1)}, bf16[4,2,128,128]{3,2,1,0:T(8,128)(2,1)S(1)}, u32[]{:S(2)}, u32[]{:S(2)}) %collective-permute-start.30) | collective-permute-done | bytes 262176 | tf_op jit(solution)/shard_map/ppermute | solution.py:779
  214.2 9.1 %project_out.1 = bf16[384,2048]{1,0:T(8,128)(2,1)} custom-call(s32[3]{0:T(128)} %copy-done.6, bf16[6,128,128]{2,1,0:T(8,128)(2,1)} %copy-done.4, bf16[6,128,128]{2,1,0:T(8,128)(2,1)} %copy-done.10, bf16[6,128,128]{2,1,0:T(8,128)(2,1)} %copy-done.11, bf16[6,128,128]{2,1,0:T(8,128)(2,1)} %copy-done.12, bf16[4,2,128,128]{3,2,1,0:T(8,128)(2,1)} %copy-done.13, ...), custom_call_target="tpu_custom_call" | custom-call | flops 3221225472 | bytes 8388608 | tf_op jit(solution)/shard_map/project_out/pallas_call | solution.py:671
  (135 shorter events, 16.8 us)
Async XLA Ops:
  6.5 206.9 %all-gather.2.cloned.1.call-start = ((), (), s32[]{:S(2)}) async-start(), calls=%async_computation | async-start | bytes 9437184 | tf_op jit(solution)/shard_map/all_gather | solution.py:766
  6.5 10.9 %collective-permute-start = (bf16[3,2048,256]{2,1,0:T(8,128)(2,1)}, bf16[3,2048,256]{2,1,0:T(8,128)(2,1)}, u32[]{:S(2)}, u32[]{:S(2)}) collective-permute-start(bf16[3,2048,256]{2,1,0:T(8,128)(2,1)} %bitcast.89), channel_id=1, source_target_pairs={{0,1},{1,0},{2,3},{3,2},{4,5},{5,4},{6,7},{7,6},{8,9},{9,8},{10,11... | collective-permute-start | bytes 9437192 | tf_op jit(solution)/shard_map/ppermute | solution.py:715
  8.8 6.3 %copy-start.5 = (s32[6,12]{1,0:T(8,128)S(1)}, s32[6,12]{1,0:T(8,128)}, u32[]{:S(2)}) copy-start(s32[6,12]{1,0:T(8,128)} %refs_0_.7) | copy-start | bytes 868
  10.4 37.7 %collective-permute-start.5 = (bf16[384,2048]{1,0:T(8,128)(2,1)}, bf16[384,2048]{1,0:T(8,128)(2,1)S(1)}, u32[]{:S(2)}, u32[]{:S(2)}) collective-permute-start(bf16[384,2048]{1,0:T(8,128)(2,1)} %fusion.2.rest_0_), channel_id=1, source_target_pairs={{0,2},{1,3},{2,0},{3,1},{4,6},{5,7},{6,4},{7,5},{8,10},{9,11},{10,... | collective-permute-start | bytes 4718600 | tf_op jit(solution)/shard_map/ppermute | solution.py:723
  13.0 36.7 %collective-permute-start.4 = (bf16[384,2048]{1,0:T(8,128)(2,1)}, bf16[384,2048]{1,0:T(8,128)(2,1)}, u32[]{:S(2)}, u32[]{:S(2)}) collective-permute-start(bf16[384,2048]{1,0:T(8,128)(2,1)} %fusion.2.rest_0_), channel_id=1, source_target_pairs={{0,4},{1,5},{2,6},{3,7},{4,0},{5,1},{6,2},{7,3},{8,12},{9,13},{10,... | collective-permute-start | bytes 4718600 | tf_op jit(solution)/shard_map/ppermute | solution.py:722
  25.3 33.1 %collective-permute-start.1 = (bf16[400,384]{1,0:T(8,128)(2,1)}, bf16[400,384]{1,0:T(8,128)(2,1)S(1)}, u32[]{:S(2)}, u32[]{:S(2)}) collective-permute-start(bf16[400,384]{1,0:T(8,128)(2,1)} %get-tuple-element.90), channel_id=1, source_target_pairs={{0,8},{8,16},{16,24},{24,0},{1,9},{9,17},{17,25},{25,1},{2,10},{10... | collective-permute-start | bytes 921608 | tf_op jit(solution)/shard_map/ppermute | solution.py:708
  27.0 31.5 %collective-permute-start.2 = (bf16[400,384]{1,0:T(8,128)(2,1)}, bf16[400,384]{1,0:T(8,128)(2,1)S(1)}, u32[]{:S(2)}, u32[]{:S(2)}) collective-permute-start(bf16[400,384]{1,0:T(8,128)(2,1)} %get-tuple-element.91), channel_id=1, source_target_pairs={{0,16},{8,24},{16,0},{24,8},{1,17},{9,25},{17,1},{25,9},{2,18},{10... | collective-permute-start | bytes 921608 | tf_op jit(solution)/shard_map/ppermute | solution.py:708
  29.6 28.9 %collective-permute-start.3 = (bf16[400,384]{1,0:T(8,128)(2,1)}, bf16[400,384]{1,0:T(8,128)(2,1)S(1)}, u32[]{:S(2)}, u32[]{:S(2)}) collective-permute-start(bf16[400,384]{1,0:T(8,128)(2,1)} %get-tuple-element.92), channel_id=1, source_target_pairs={{0,24},{8,0},{16,8},{24,16},{1,25},{9,1},{17,9},{25,17},{2,26},{10... | collective-permute-start | bytes 921608 | tf_op jit(solution)/shard_map/ppermute | solution.py:708
  58.5 19.3 %collective-permute-start.10 = (bf16[192,2048]{1,0:T(8,128)(2,1)}, bf16[192,2048]{1,0:T(8,128)(2,1)S(1)}, u32[]{:S(2)}, u32[]{:S(2)}) collective-permute-start(bf16[192,2048]{1,0:T(8,128)(2,1)} %get-tuple-element.109), channel_id=1, source_target_pairs={{0,4},{1,5},{2,6},{3,7},{4,0},{5,1},{6,2},{7,3},{8,12},{9,13},{10,... | collective-permute-start | bytes 2359304 | tf_op jit(solution)/shard_map/ppermute | solution.py:757
  60.1 18.9 %collective-permute-start.9 = (bf16[192,2048]{1,0:T(8,128)(2,1)}, bf16[192,2048]{1,0:T(8,128)(2,1)S(1)}, u32[]{:S(2)}, u32[]{:S(2)}) collective-permute-start(bf16[192,2048]{1,0:T(8,128)(2,1)} %get-tuple-element.108), channel_id=1, source_target_pairs={{0,2},{1,3},{2,0},{3,1},{4,6},{5,7},{6,4},{7,5},{8,10},{9,11},{10,... | collective-permute-start | bytes 2359304 | tf_op jit(solution)/shard_map/ppermute | solution.py:756
  62.2 26.6 %collective-permute-start.6 = (bf16[384,384]{1,0:T(8,128)(2,1)}, bf16[384,384]{1,0:T(8,128)(2,1)S(1)}, u32[]{:S(2)}, u32[]{:S(2)}) collective-permute-start(bf16[384,384]{1,0:T(8,128)(2,1)} %get-tuple-element.105), channel_id=1, source_target_pairs={{0,8},{8,16},{16,24},{24,0},{1,9},{9,17},{17,25},{25,1},{2,10},{10... | collective-permute-start | bytes 884744 | tf_op jit(solution)/shard_map/ppermute | solution.py:708
  63.8 25.0 %collective-permute-start.7 = (bf16[384,384]{1,0:T(8,128)(2,1)}, bf16[384,384]{1,0:T(8,128)(2,1)S(1)}, u32[]{:S(2)}, u32[]{:S(2)}) collective-permute-start(bf16[384,384]{1,0:T(8,128)(2,1)} %get-tuple-element.106), channel_id=1, source_target_pairs={{0,16},{8,24},{16,0},{24,8},{1,17},{9,25},{17,1},{25,9},{2,18},{10... | collective-permute-start | bytes 884744 | tf_op jit(solution)/shard_map/ppermute | solution.py:708
  66.4 22.4 %collective-permute-start.8 = (bf16[384,384]{1,0:T(8,128)(2,1)}, bf16[384,384]{1,0:T(8,128)(2,1)S(1)}, u32[]{:S(2)}, u32[]{:S(2)}) collective-permute-start(bf16[384,384]{1,0:T(8,128)(2,1)} %get-tuple-element.107), channel_id=1, source_target_pairs={{0,24},{8,0},{16,8},{24,16},{1,25},{9,1},{17,9},{25,17},{2,26},{10... | collective-permute-start | bytes 884744 | tf_op jit(solution)/shard_map/ppermute | solution.py:708
  90.5 6.4 %copy-start.1 = (bf16[384,384]{1,0:T(8,128)(2,1)S(1)}, bf16[384,384]{1,0:T(8,128)(2,1)}, u32[]{:S(2)}) copy-start(bf16[384,384]{1,0:T(8,128)(2,1)} %get-tuple-element.127.refs_8_.refs_12_) | copy-start | bytes 884740
  90.7 33.3 %collective-permute-start.17 = (bf16[4,400,384]{2,1,0:T(8,128)(2,1)S(1)}, bf16[4,400,384]{2,1,0:T(8,128)(2,1)S(1)}, u32[]{:S(2)}, u32[]{:S(2)}) collective-permute-start(bf16[4,400,384]{2,1,0:T(8,128)(2,1)S(1)} %pad_maximum_fusion), channel_id=1, source_target_pairs={{0,1},{1,0},{2,3},{3,2},{4,5},{5,4},{6,7},{7,6},{8,9},{9,8},{10,11... | collective-permute-start | bytes 3686408 | tf_op jit(solution)/shard_map/ppermute | solution.py:740
  91.5 15.8 %collective-permute-start.11 = (bf16[384,384]{1,0:T(8,128)(2,1)S(1)}, bf16[384,384]{1,0:T(8,128)(2,1)S(1)}, u32[]{:S(2)}, u32[]{:S(2)}) collective-permute-start(bf16[384,384]{1,0:T(8,128)(2,1)S(1)} %copy-done.22), channel_id=1, source_target_pairs={{0,8},{8,16},{16,24},{24,0},{1,9},{9,17},{17,25},{25,1},{2,10},{10... | collective-permute-start | bytes 884744 | tf_op jit(solution)/shard_map/ppermute | solution.py:708
  94.5 20.8 %collective-permute-start.12 = (bf16[384,384]{1,0:T(8,128)(2,1)S(1)}, bf16[384,384]{1,0:T(8,128)(2,1)S(1)}, u32[]{:S(2)}, u32[]{:S(2)}) collective-permute-start(bf16[384,384]{1,0:T(8,128)(2,1)S(1)} %copy-done.20), channel_id=1, source_target_pairs={{0,16},{8,24},{16,0},{24,8},{1,17},{9,25},{17,1},{25,9},{2,18},{10... | collective-permute-start | bytes 884744 | tf_op jit(solution)/shard_map/ppermute | solution.py:708
  96.1 19.2 %collective-permute-start.13 = (bf16[384,384]{1,0:T(8,128)(2,1)S(1)}, bf16[384,384]{1,0:T(8,128)(2,1)S(1)}, u32[]{:S(2)}, u32[]{:S(2)}) collective-permute-start(bf16[384,384]{1,0:T(8,128)(2,1)S(1)} %copy-done.19), channel_id=1, source_target_pairs={{0,24},{8,0},{16,8},{24,16},{1,25},{9,1},{17,9},{25,17},{2,26},{10... | collective-permute-start | bytes 884744 | tf_op jit(solution)/shard_map/ppermute | solution.py:708
  98.1 17.1 %copy-start.2 = (bf16[384,384]{1,0:T(8,128)(2,1)S(1)}, bf16[384,384]{1,0:T(8,128)(2,1)}, u32[]{:S(2)}) copy-start(bf16[384,384]{1,0:T(8,128)(2,1)} %get-tuple-element.131.refs_12_.refs_16_) | copy-start | bytes 884740
  98.1 26.9 %collective-permute-start.18 = (bf16[4,384,384]{2,1,0:T(8,128)(2,1)}, bf16[4,384,384]{2,1,0:T(8,128)(2,1)S(1)}, u32[]{:S(2)}, u32[]{:S(2)}) collective-permute-start(bf16[4,384,384]{2,1,0:T(8,128)(2,1)} %pad_maximum_fusion.1), channel_id=1, source_target_pairs={{0,1},{1,0},{2,3},{3,2},{4,5},{5,4},{6,7},{7,6},{8,9},{9,8},{10,11... | collective-permute-start | bytes 3538952 | tf_op jit(solution)/shard_map/ppermute | solution.py:740
  107.2 8.4 %copy-start.24 = (bf16[384,384]{1,0:T(8,128)(2,1)S(1)}, bf16[384,384]{1,0:T(8,128)(2,1)}, u32[]{:S(2)}) copy-start(bf16[384,384]{1,0:T(8,128)(2,1)} %get-tuple-element.124) | copy-start | bytes 884740
  107.2 15.4 %copy-start.23 = (bf16[384,384]{1,0:T(8,128)(2,1)S(1)}, bf16[384,384]{1,0:T(8,128)(2,1)}, u32[]{:S(2)}) copy-start(bf16[384,384]{1,0:T(8,128)(2,1)} %get-tuple-element.125) | copy-start | bytes 884740
  107.2 16.8 %copy-start.21 = (bf16[384,384]{1,0:T(8,128)(2,1)S(1)}, bf16[384,384]{1,0:T(8,128)(2,1)}, u32[]{:S(2)}) copy-start(bf16[384,384]{1,0:T(8,128)(2,1)} %get-tuple-element.126) | copy-start | bytes 884740
  115.5 9.6 %collective-permute-start.19 = (bf16[4,384,384]{2,1,0:T(8,128)(2,1)S(1)}, bf16[4,384,384]{2,1,0:T(8,128)(2,1)S(1)}, u32[]{:S(2)}, u32[]{:S(2)}) collective-permute-start(bf16[4,384,384]{2,1,0:T(8,128)(2,1)S(1)} %pad_maximum_fusion.2), channel_id=1, source_target_pairs={{0,1},{1,0},{2,3},{3,2},{4,5},{5,4},{6,7},{7,6},{8,9},{9,8},{10,11... | collective-permute-start | bytes 3538952 | tf_op jit(solution)/shard_map/ppermute | solution.py:740
  115.6 73.9 %copy-start.6 = (s32[3]{0:T(128)}, s32[3]{0:T(128)S(1)}, u32[]{:S(2)}) copy-start(s32[3]{0:T(128)S(1)} %pad_add_fusion.place) | copy-start | bytes 40
  115.6 27.0 %collective-permute-start.14 = (bf16[384,384]{1,0:T(8,128)(2,1)S(1)}, bf16[384,384]{1,0:T(8,128)(2,1)S(1)}, u32[]{:S(2)}, u32[]{:S(2)}) collective-permute-start(bf16[384,384]{1,0:T(8,128)(2,1)S(1)} %copy-done.24), channel_id=1, source_target_pairs={{0,8},{8,16},{16,24},{24,0},{1,9},{9,17},{17,25},{25,1},{2,10},{10... | collective-permute-start | bytes 884744 | tf_op jit(solution)/shard_map/ppermute | solution.py:708
  122.6 21.2 %collective-permute-start.15 = (bf16[384,384]{1,0:T(8,128)(2,1)S(1)}, bf16[384,384]{1,0:T(8,128)(2,1)S(1)}, u32[]{:S(2)}, u32[]{:S(2)}) collective-permute-start(bf16[384,384]{1,0:T(8,128)(2,1)S(1)} %copy-done.23), channel_id=1, source_target_pairs={{0,16},{8,24},{16,0},{24,8},{1,17},{9,25},{17,1},{25,9},{2,18},{10... | collective-permute-start | bytes 884744 | tf_op jit(solution)/shard_map/ppermute | solution.py:708
  124.0 19.9 %collective-permute-start.16 = (bf16[384,384]{1,0:T(8,128)(2,1)S(1)}, bf16[384,384]{1,0:T(8,128)(2,1)S(1)}, u32[]{:S(2)}, u32[]{:S(2)}) collective-permute-start(bf16[384,384]{1,0:T(8,128)(2,1)S(1)} %copy-done.21), channel_id=1, source_target_pairs={{0,24},{8,0},{16,8},{24,16},{1,25},{9,1},{17,9},{25,17},{2,26},{10... | collective-permute-start | bytes 884744 | tf_op jit(solution)/shard_map/ppermute | solution.py:708
  125.1 18.8 %copy-start.3 = (bf16[384,384]{1,0:T(8,128)(2,1)S(1)}, bf16[384,384]{1,0:T(8,128)(2,1)}, u32[]{:S(2)}) copy-start(bf16[384,384]{1,0:T(8,128)(2,1)} %get-tuple-element.138.refs_8_) | copy-start | bytes 884740
  143.8 1.6 collective-permute-start.20
  143.9 2.0 collective-permute-start.21
  144.4 1.9 collective-permute-start.22
  144.4 2.3 collective-permute-start.23
  157.9 24.9 %collective-permute-start.24 = (bf16[6,128,128]{2,1,0:T(8,128)(2,1)S(1)}, bf16[6,128,128]{2,1,0:T(8,128)(2,1)S(1)}, u32[]{:S(2)}, u32[]{:S(2)}) collective-permute-start(bf16[6,128,128]{2,1,0:T(8,128)(2,1)S(1)} %get-tuple-element.149), channel_id=1, source_target_pairs={{0,8},{8,16},{16,24},{24,0},{1,9},{9,17},{17,25},{25,1},{2,10},{10... | collective-permute-start | bytes 589832 | tf_op jit(solution)/shard_map/ppermute | solution.py:708
  164.7 18.0 %collective-permute-start.25 = (bf16[6,128,128]{2,1,0:T(8,128)(2,1)S(1)}, bf16[6,128,128]{2,1,0:T(8,128)(2,1)S(1)}, u32[]{:S(2)}, u32[]{:S(2)}) collective-permute-start(bf16[6,128,128]{2,1,0:T(8,128)(2,1)S(1)} %get-tuple-element.150), channel_id=1, source_target_pairs={{0,16},{8,24},{16,0},{24,8},{1,17},{9,25},{17,1},{25,9},{2,18},{10... | collective-permute-start | bytes 589832 | tf_op jit(solution)/shard_map/ppermute | solution.py:708
  166.1 16.6 %collective-permute-start.26 = (bf16[6,128,128]{2,1,0:T(8,128)(2,1)S(1)}, bf16[6,128,128]{2,1,0:T(8,128)(2,1)S(1)}, u32[]{:S(2)}, u32[]{:S(2)}) collective-permute-start(bf16[6,128,128]{2,1,0:T(8,128)(2,1)S(1)} %get-tuple-element.151), channel_id=1, source_target_pairs={{0,24},{8,0},{16,8},{24,16},{1,25},{9,1},{17,9},{25,17},{2,26},{10... | collective-permute-start | bytes 589832 | tf_op jit(solution)/shard_map/ppermute | solution.py:708
  182.9 19.5 %collective-permute-start.32 = (bf16[4,3,128,128]{3,2,0,1:T(8,128)(2,1)S(1)}, bf16[4,3,128,128]{3,2,0,1:T(8,128)(2,1)S(1)}, u32[]{:S(2)}, u32[]{:S(2)}) collective-permute-start(bf16[4,3,128,128]{3,2,0,1:T(8,128)(2,1)S(1)} %pad_maximum_fusion.4), channel_id=1, source_target_pairs={{0,6},{1,7},{2,4},{3,5},{4,2},{5,3},{6,0},{7,1},{8,14},{9,15},{10,... | collective-permute-start | bytes 1179656 | tf_op jit(solution)/shard_map/ppermute | solution.py:779
  184.8 18.1 %collective-permute-start.31 = (bf16[4,3,128,128]{3,2,1,0:T(8,128)(2,1)S(1)}, bf16[4,3,128,128]{3,2,1,0:T(8,128)(2,1)S(1)}, u32[]{:S(2)}, u32[]{:S(2)}) collective-permute-start(bf16[4,3,128,128]{3,2,1,0:T(8,128)(2,1)S(1)} %pad_maximum_fusion.3), channel_id=1, source_target_pairs={{0,4},{1,5},{2,6},{3,7},{4,0},{5,1},{6,2},{7,3},{8,12},{9,13},{10,... | collective-permute-start | bytes 1179656 | tf_op jit(solution)/shard_map/ppermute | solution.py:779
  185.7 9.8 %collective-permute-start.27 = (bf16[6,128,128]{2,1,0:T(8,128)(2,1)S(1)}, bf16[6,128,128]{2,1,0:T(8,128)(2,1)S(1)}, u32[]{:S(2)}, u32[]{:S(2)}) collective-permute-start(bf16[6,128,128]{2,1,0:T(8,128)(2,1)S(1)} %get-tuple-element.153), channel_id=1, source_target_pairs={{0,8},{8,16},{16,24},{24,0},{1,9},{9,17},{17,25},{25,1},{2,10},{10... | collective-permute-start | bytes 589832 | tf_op jit(solution)/shard_map/ppermute | solution.py:708
  186.8 15.0 %collective-permute-start.28 = (bf16[6,128,128]{2,1,0:T(8,128)(2,1)S(1)}, bf16[6,128,128]{2,1,0:T(8,128)(2,1)S(1)}, u32[]{:S(2)}, u32[]{:S(2)}) collective-permute-start(bf16[6,128,128]{2,1,0:T(8,128)(2,1)S(1)} %get-tuple-element.154), channel_id=1, source_target_pairs={{0,16},{8,24},{16,0},{24,8},{1,17},{9,25},{17,1},{25,9},{2,18},{10... | collective-permute-start | bytes 589832 | tf_op jit(solution)/shard_map/ppermute | solution.py:708
  188.4 13.5 %collective-permute-start.29 = (bf16[6,128,128]{2,1,0:T(8,128)(2,1)S(1)}, bf16[6,128,128]{2,1,0:T(8,128)(2,1)S(1)}, u32[]{:S(2)}, u32[]{:S(2)}) collective-permute-start(bf16[6,128,128]{2,1,0:T(8,128)(2,1)S(1)} %get-tuple-element.155), channel_id=1, source_target_pairs={{0,24},{8,0},{16,8},{24,16},{1,25},{9,1},{17,9},{25,17},{2,26},{10... | collective-permute-start | bytes 589832 | tf_op jit(solution)/shard_map/ppermute | solution.py:708
  194.9 8.4 %copy-start.4 = (bf16[6,128,128]{2,1,0:T(8,128)(2,1)}, bf16[6,128,128]{2,1,0:T(8,128)(2,1)S(1)}, u32[]{:S(2)}) copy-start(bf16[6,128,128]{2,1,0:T(8,128)(2,1)S(1)} %attend_local.1.rest_0_) | copy-start | bytes 589828
  195.5 7.8 %copy-start.10 = (bf16[6,128,128]{2,1,0:T(8,128)(2,1)}, bf16[6,128,128]{2,1,0:T(8,128)(2,1)S(1)}, u32[]{:S(2)}) copy-start(bf16[6,128,128]{2,1,0:T(8,128)(2,1)S(1)} %collective-permute-done.27.rest_1_) | copy-start | bytes 589828
  201.9 5.8 %collective-permute-start.34 = (bf16[4,1,128,128]{3,2,1,0:T(8,128)(2,1)S(1)}, bf16[4,1,128,128]{3,2,1,0:T(8,128)(2,1)S(1)}, u32[]{:S(2)}, u32[]{:S(2)}) collective-permute-start(bf16[4,1,128,128]{3,2,1,0:T(8,128)(2,1)S(1)} %pad_maximum_fusion.16), channel_id=1, source_target_pairs={{0,3},{1,2},{2,1},{3,0},{4,7},{5,6},{6,5},{7,4},{8,11},{9,10},{10,... | collective-permute-start | bytes 393224 | tf_op jit(solution)/shard_map/ppermute | solution.py:779
  203.0 2.4 %collective-permute-start.35 = (bf16[2,4,1,128,128]{4,3,1,2,0:T(8,128)(2,1)S(1)}, bf16[2,4,1,128,128]{4,3,1,2,0:T(8,128)(2,1)S(1)}, u32[]{:S(2)}, u32[]{:S(2)}) collective-permute-start(bf16[2,4,1,128,128]{4,3,1,2,0:T(8,128)(2,1)S(1)} %pad_maximum_fusion.6), channel_id=1, source_target_pairs={{0,1},{1,0},{2,3},{3,2},{4,5},{5,4},{6,7},{7,6},{8,9},{9,8},{10,11... | collective-permute-start | bytes 786440 | tf_op jit(solution)/shard_map/ppermute | solution.py:740
  203.3 10.1 %collective-permute-start.30 = (bf16[4,2,128,128]{3,2,1,0:T(8,128)(2,1)S(1)}, bf16[4,2,128,128]{3,2,1,0:T(8,128)(2,1)S(1)}, u32[]{:S(2)}, u32[]{:S(2)}) collective-permute-start(bf16[4,2,128,128]{3,2,1,0:T(8,128)(2,1)S(1)} %pad_maximum_fusion.5), channel_id=1, source_target_pairs={{0,2},{1,3},{2,0},{3,1},{4,6},{5,7},{6,4},{7,5},{8,10},{9,11},{10,... | collective-permute-start | bytes 786440 | tf_op jit(solution)/shard_map/ppermute | solution.py:779
  204.5 3.2 %collective-permute-start.33 = (bf16[4,1,128,128]{3,2,1,0:T(8,128)(2,1)S(1)}, bf16[4,1,128,128]{3,2,1,0:T(8,128)(2,1)S(1)}, u32[]{:S(2)}, u32[]{:S(2)}) collective-permute-start(bf16[4,1,128,128]{3,2,1,0:T(8,128)(2,1)S(1)} %pad_maximum_fusion.15), channel_id=1, source_target_pairs={{0,1},{1,0},{2,3},{3,2},{4,5},{5,4},{6,7},{7,6},{8,9},{9,8},{10,11... | collective-permute-start | bytes 393224 | tf_op jit(solution)/shard_map/ppermute | solution.py:740
  207.7 5.7 %copy-start.14 = (bf16[4,1,128,128]{3,2,1,0:T(8,128)(2,1)}, bf16[4,1,128,128]{3,2,1,0:T(8,128)(2,1)S(1)}, u32[]{:S(2)}) copy-start(bf16[4,1,128,128]{3,2,1,0:T(8,128)(2,1)S(1)} %collective-permute-done.34.rest_8_) | copy-start | bytes 393220
  (14 other events, 33.4 us)
Sparse Core Ops, SparseCore 0:
  89.0 55.2 all-gather.1
where the time goes:
time: 232 us; the launch traced here: 230 us
  Pallas kernels  93.2 us (40%)
  starting transfers between devices  52.6 us (23%)
  waiting for transfers between devices  51.2 us (22%)
  other arithmetic  14.5 us (6%)
  between operations  13.9 us (6%)
  local copies, waits for them, and re-layouts  4.59 us (2%)
    pallas_call x4, Pallas kernels, attend(): pl.pallas_call(functools.partial(attend_kernel, mode, blocks_here), out_s...  49.6 us
    ppermute x18, starting transfers between devices, to_section(): lax.ppermute(array, 'section', [(i, (i + shift) % 4) for i in range(4)])  39.2 us
    pallas_call x4, Pallas kernels, project(): pl.pallas_call(functools.partial(project_kernel, number, len(notes) > 0,...  34.6 us
    ppermute x18, waiting for transfers between devices, to_section(): lax.ppermute(array, 'section', [(i, (i + shift) % 4) for i in range(4)])  16.2 us
    ppermute x1, waiting for transfers between devices, by_head(): x_rows = lax.ppermute(normed, 'head', along_x)  13.5 us
    ppermute x1, waiting for transfers between devices, by_head(): d_high = lax.ppermute(x_high, 'head', along_y)  9.17 us
    pallas_call x1, Pallas kernels, finish(): pl.pallas_call(functools.partial(finish_kernel, relatives, [len(parts) fo...  9.09 us
    ppermute x4, waiting for transfers between devices, to_chip(): return lax.ppermute(array, 'head', [(i, i ^ flip) for i in range(8)])  7.72 us
  transfers between devices with their start and end apart: 37, of which 15 were waited for; matrix products, arithmetic and copies ran while one was open for 7% of the time, Pallas kernels for 37%

commit v1 on v0

--- a/solution.py
+++ b/solution.py
@@ -12,7 +12,7 @@
 HD = 128
 BLK = 512
 TILE = 128
-STEPS = {"early": 4, "late": 12, "near": 12, "local": 3}
+STEPS = {"early": 4, "late": 8, "near": 12, "local": 3}
 
 
 EPS = 1e-05

time: 232 us -> 232 us (level)
  transfers between devices with their start and end apart: 37 -> 37, of which waited for: 15 -> 15; matrix products, arithmetic and copies ran while one was open for 7% -> 7% of each run, Pallas kernels for 37% -> 36%
where the time goes in v1:
time: 232 us; the launch traced here: 230 us
  Pallas kernels  92.9 us (40%)
  starting transfers between devices  52.7 us (23%)
  waiting for transfers between devices  51.1 us (22%)
  other arithmetic  14.5 us (6%)
  between operations  13.9 us (6%)
  local copies, waits for them, and re-layouts  4.59 us (2%)
    pallas_call x4, Pallas kernels, attend(): pl.pallas_call(functools.partial(attend_kernel, mode, blocks_here), out_s...  49.3 us
    ppermute x18, starting transfers between devices, to_section(): lax.ppermute(array, 'section', [(i, (i + shift) % 4) for i in range(4)])  39.1 us
    pallas_call x4, Pallas kernels, project(): pl.pallas_call(functools.partial(project_kernel, number, len(notes) > 0,...  34.6 us
    ppermute x18, waiting for transfers between devices, to_section(): lax.ppermute(array, 'section', [(i, (i + shift) % 4) for i in range(4)])  16.2 us
    ppermute x1, waiting for transfers between devices, by_head(): x_rows = lax.ppermute(normed, 'head', along_x)  13.5 us
    ppermute x1, waiting for transfers between devices, by_head(): d_high = lax.ppermute(x_high, 'head', along_y)  9.17 us
    pallas_call x1, Pallas kernels, finish(): pl.pallas_call(functools.partial(finish_kernel, relatives, [len(parts) fo...  9.09 us
    ppermute x4, waiting for transfers between devices, to_chip(): return lax.ppermute(array, 'head', [(i, i ^ flip) for i in range(8)])  7.65 us
  transfers between devices with their start and end apart: 37, of which 15 were waited for; matrix products, arithmetic and copies ran while one was open for 7% of the time, Pallas kernels for 36%

profile of v1, /device:TPU:0, one launch (start us, length us, event | category | flops | bytes accessed | tf_op | source)
XLA Modules:
  0.0 229.8 jit_solution(4291259610958561819)
XLA Ops:
  7.0 1.8 fusion
  8.9 1.6 fusion.2.rest_0_
  10.4 2.6 %collective-permute-start.5 = (bf16[384,2048]{1,0:T(8,128)(2,1)}, bf16[384,2048]{1,0:T(8,128)(2,1)S(1)}, u32[]{:S(2)}, u32[]{:S(2)}) collective-permute-start(bf16[384,2048]{1,0:T(8,128)(2,1)} %fusion.2.rest_0_), channel_id=1, source_target_pairs={{0,2},{1,3},{2,0},{3,1},{4,6},{5,7},{6,4},{7,5},{8,10},{9,11},{10,... | collective-permute-start | bytes 4718600 | tf_op jit(solution)/shard_map/ppermute | solution.py:723
  13.0 1.5 collective-permute-start.4
  16.5 0.9 pad_maximum_fusion.7
  17.5 7.8 %project_and_rotate.4 = (bf16[400,384]{1,0:T(8,128)(2,1)}, bf16[400,384]{1,0:T(8,128)(2,1)}, bf16[400,384]{1,0:T(8,128)(2,1)}, bf16[400,384]{1,0:T(8,128)(2,1)}) custom-call(s32[4]{0:T(128)} %and_select_fusion.place, bf16[384,2048]{1,0:T(8,128)(2,1)} %fusion.2.rest_0_, bf16[16,384]{1,0:T(8,128)(2,1)} %pad.4.rest_1_, bf16[3,2048,256]{2,1,0:T(8,128)(2,1)} %bitcast.90, ...), custom_call_target="tpu_custom_call" | custom-call | flops 2415919104 | bytes 6291456 | tf_op jit(solution)/shard_map/project_and_rotate/pallas_call | solution.py:235
  25.3 1.6 collective-permute-start.1
  27.0 2.6 %collective-permute-start.2 = (bf16[400,384]{1,0:T(8,128)(2,1)}, bf16[400,384]{1,0:T(8,128)(2,1)S(1)}, u32[]{:S(2)}, u32[]{:S(2)}) collective-permute-start(bf16[400,384]{1,0:T(8,128)(2,1)} %get-tuple-element.91), channel_id=1, source_target_pairs={{0,16},{8,24},{16,0},{24,8},{1,17},{9,25},{17,1},{25,9},{2,18},{10... | collective-permute-start | bytes 921608 | tf_op jit(solution)/shard_map/ppermute | solution.py:708
  29.6 1.4 collective-permute-start.3
  30.9 2.1 fusion.6
  34.7 13.5 %collective-permute-done.5.rest_1_.rest_0_ = bf16[384,2048]{1,0:T(8,128)(2,1)S(1)} collective-permute-done((bf16[384,2048]{1,0:T(8,128)(2,1)}, bf16[384,2048]{1,0:T(8,128)(2,1)S(1)}, u32[]{:S(2)}, u32[]{:S(2)}) %collective-permute-start.5) | collective-permute-done | bytes 1572896 | tf_op jit(solution)/shard_map/ppermute | solution.py:723
  48.2 1.6 collective-permute-done.4.rest_0_
  49.7 8.7 %project_and_rotate.5 = (bf16[384,384]{1,0:T(8,128)(2,1)}, bf16[384,384]{1,0:T(8,128)(2,1)}, bf16[384,384]{1,0:T(8,128)(2,1)}, bf16[384,384]{1,0:T(8,128)(2,1)},...) custom-call(s32[4]{0:T(128)} %and_select_fusion.place, bf16[384,2048]{1,0:T(8,128)(2,1)} %collective-permute-done.4.rest_0_, ...), custom_call_target="tpu_custom_call" | custom-call | flops 2415919104 | bytes 6291456 | tf_op jit(solution)/shard_map/project_and_rotate/pallas_call | solution.py:235
  58.5 1.6 collective-permute-start.10
  60.1 1.3 collective-permute-start.9
  62.2 1.6 collective-permute-start.6
  63.8 2.6 %collective-permute-start.7 = (bf16[384,384]{1,0:T(8,128)(2,1)}, bf16[384,384]{1,0:T(8,128)(2,1)S(1)}, u32[]{:S(2)}, u32[]{:S(2)}) collective-permute-start(bf16[384,384]{1,0:T(8,128)(2,1)} %get-tuple-element.106), channel_id=1, source_target_pairs={{0,16},{8,24},{16,0},{24,8},{1,17},{9,25},{17,1},{25,9},{2,18},{10... | collective-permute-start | bytes 884744 | tf_op jit(solution)/shard_map/ppermute | solution.py:708
  66.4 1.3 collective-permute-start.8
  68.6 9.2 %collective-permute-done.10.rest_1_ = bf16[192,2048]{1,0:T(8,128)(2,1)S(1)} collective-permute-done((bf16[192,2048]{1,0:T(8,128)(2,1)}, bf16[192,2048]{1,0:T(8,128)(2,1)S(1)}, u32[]{:S(2)}, u32[]{:S(2)}) %collective-permute-start.10) | collective-permute-done | bytes 786464 | tf_op jit(solution)/shard_map/ppermute | solution.py:757
  77.8 1.2 collective-permute-done.9.rest_0_
  79.0 0.9 copy-done.18
  79.9 9.0 %project_and_rotate.6 = (bf16[384,384]{1,0:T(8,128)(2,1)}, bf16[384,384]{1,0:T(8,128)(2,1)}, bf16[384,384]{1,0:T(8,128)(2,1)}, bf16[384,384]{1,0:T(8,128)(2,1)}) custom-call(s32[4]{0:T(128)} %and_select_fusion.place, bf16[192,2048]{1,0:T(8,128)(2,1)} %copy-done.18, bf16[192,2048]{1,0:T(8,128)(2,1)} %copy-done.17, bf16[3,2048,256]{2,1,0:T(8,128)(2,1)} %bitcast.92, ...), custom_call_target="tpu_custom_call" | custom-call | flops 2415919104 | bytes 6291456 | tf_op jit(solution)/shard_map/project_and_rotate/pallas_call | solution.py:235
  91.5 3.0 %collective-permute-start.11 = (bf16[384,384]{1,0:T(8,128)(2,1)S(1)}, bf16[384,384]{1,0:T(8,128)(2,1)S(1)}, u32[]{:S(2)}, u32[]{:S(2)}) collective-permute-start(bf16[384,384]{1,0:T(8,128)(2,1)S(1)} %copy-done.22), channel_id=1, source_target_pairs={{0,8},{8,16},{16,24},{24,0},{1,9},{9,17},{17,25},{25,1},{2,10},{10... | collective-permute-start | bytes 884744 | tf_op jit(solution)/shard_map/ppermute | solution.py:708
  94.5 1.6 collective-permute-start.12
  96.9 1.2 pad_maximum_fusion.1
  98.1 9.1 %project_and_rotate.7 = (bf16[384,384]{1,0:T(8,128)(2,1)}, bf16[384,384]{1,0:T(8,128)(2,1)}, bf16[384,384]{1,0:T(8,128)(2,1)}, bf16[384,384]{1,0:T(8,128)(2,1)}) custom-call(s32[4]{0:T(128)} %and_select_fusion.place, bf16[384,2048]{1,0:T(8,128)(2,1)} %copy-done.8, bf16[3,2048,256]{2,1,0:T(8,128)(2,1)} %bitcast.93, ...), custom_call_target="tpu_custom_call" | custom-call | flops 2415919104 | bytes 6291456 | tf_op jit(solution)/shard_map/project_and_rotate/pallas_call | solution.py:235
  107.2 8.0 %collective-permute-done.12.refs_14_.refs_18_ = bf16[384,384]{1,0:T(8,128)(2,1)S(1)} collective-permute-done((bf16[384,384]{1,0:T(8,128)(2,1)S(1)}, bf16[384,384]{1,0:T(8,128)(2,1)S(1)}, u32[]{:S(2)}, u32[]{:S(2)}) %collective-permute-start.12) | collective-permute-done | bytes 294944 | tf_op jit(solution)/shard_map/ppermute | solution.py:708
  115.6 7.0 %collective-permute-start.14 = (bf16[384,384]{1,0:T(8,128)(2,1)S(1)}, bf16[384,384]{1,0:T(8,128)(2,1)S(1)}, u32[]{:S(2)}, u32[]{:S(2)}) collective-permute-start(bf16[384,384]{1,0:T(8,128)(2,1)S(1)} %copy-done.24), channel_id=1, source_target_pairs={{0,8},{8,16},{16,24},{24,0},{1,9},{9,17},{17,25},{25,1},{2,10},{10... | collective-permute-start | bytes 884744 | tf_op jit(solution)/shard_map/ppermute | solution.py:708
  122.6 1.4 collective-permute-start.15
  124.0 1.1 collective-permute-start.16
  125.1 17.5 %attend_early.1 = (bf16[13,256,128]{2,1,0:T(8,128)(2,1)S(1)}, f32[13,8,256]{2,1,0:T(8,128)S(1)}, f32[13,144,256]{2,1,0:T(8,128)S(1)}) custom-call(s32[3]{0:T(128)S(1)} %pad_add_fusion.place, s32[6,12]{1,0:T(8,128)S(1)} %copy-done.5, s32[6,12]{1,0:T(8,128)S(1)} %slice_convert_fusion.2.refs_1_, s32[6,12]{1,0:T(8,128)S(1)} %slice_convert_fusion.1.refs_2_, ...), custom_call_target="tpu_custom_call" | custom-call | flops 2415919104 | bytes 7864320 | tf_op jit(solution)/shard_map/attend_early/pallas_call | solution.py:569
  142.6 1.2 collective-permute-done.15.refs_10_
  146.7 10.9 %attend_late.1 = (bf16[6,128,128]{2,1,0:T(8,128)(2,1)S(1)}, bf16[6,128,128]{2,1,0:T(8,128)(2,1)S(1)}, bf16[6,128,128]{2,1,0:T(8,128)(2,1)S(1)}, bf16[6,128,128]{2,1,0:T(8,128)(2,1)S(1)}) custom-call(s32[3]{0:T(128)S(1)} %pad_add_fusion.place, s32[6,12]{1,0:T(8,128)S(1)} %copy-done.5, s32[6,12]{1,0:T(8,128)S(1)} %slice_convert_fusion.2.refs_1_, ...), custom_call_target="tpu_custom_call" | custom-call | flops 2415919104 | bytes 7864320 | tf_op jit(solution)/shard_map/attend_late/pallas_call | solution.py:569
  157.6 6.8 %collective-permute-start.24 = (bf16[6,128,128]{2,1,0:T(8,128)(2,1)S(1)}, bf16[6,128,128]{2,1,0:T(8,128)(2,1)S(1)}, u32[]{:S(2)}, u32[]{:S(2)}) collective-permute-start(bf16[6,128,128]{2,1,0:T(8,128)(2,1)S(1)} %get-tuple-element.149), channel_id=1, source_target_pairs={{0,8},{8,16},{16,24},{24,0},{1,9},{9,17},{17,25},{25,1},{2,10},{10... | collective-permute-start | bytes 589832 | tf_op jit(solution)/shard_map/ppermute | solution.py:708
  164.4 1.4 collective-permute-start.25
  165.8 1.0 collective-permute-start.26
  166.8 15.5 %attend_near.1 = (bf16[6,128,128]{2,1,0:T(8,128)(2,1)S(1)}, bf16[6,128,128]{2,1,0:T(8,128)(2,1)S(1)}, bf16[6,128,128]{2,1,0:T(8,128)(2,1)S(1)}) custom-call(s32[3]{0:T(128)S(1)} %pad_add_fusion.place, s32[6,12]{1,0:T(8,128)S(1)} %copy-done.5, s32[6,12]{1,0:T(8,128)S(1)} %slice_convert_fusion.2.refs_1_, s32[6,12]{1,0:T(8,128)S(1)} %slice_convert_fusion.1.refs_2_, ...), custom_call_target="tpu_custom_call" | custom-call | flops 2415919104 | bytes 7864320 | tf_op jit(solution)/shard_map/attend_near/pallas_call | solution.py:569
  182.6 1.1 collective-permute-start.32
  183.7 1.6 collective-permute-start.31
  185.3 1.2 collective-permute-start.27
  186.5 1.6 collective-permute-start.28
  188.1 1.1 collective-permute-start.29
  189.2 5.4 %attend_local.1.rest_0_ = bf16[6,128,128]{2,1,0:T(8,128)(2,1)S(1)} custom-call(s32[3]{0:T(128)S(1)} %pad_add_fusion.place, s32[6,12]{1,0:T(8,128)S(1)} %copy-done.5, s32[6,12]{1,0:T(8,128)S(1)} %slice_convert_fusion.2.refs_1_, s32[6,12]{1,0:T(8,128)S(1)} %slice_convert_fusion.1.refs_2_, s32[6,12]{1,0:T(8,128)S(1)} %slice_convert_fusion.refs_3_, ...), custom_call_target="tpu_custom_call" | custom-call | flops 2415919104 | bytes 7864320 | tf_op jit(solution)/shard_map/attend_local/pallas_call | solution.py:569
  195.1 6.4 %collective-permute-done.28.rest_2_ = bf16[6,128,128]{2,1,0:T(8,128)(2,1)S(1)} collective-permute-done((bf16[6,128,128]{2,1,0:T(8,128)(2,1)S(1)}, bf16[6,128,128]{2,1,0:T(8,128)(2,1)S(1)}, u32[]{:S(2)}, u32[]{:S(2)}) %collective-permute-start.28) | collective-permute-done | bytes 196640 | tf_op jit(solution)/shard_map/ppermute | solution.py:708
  203.0 1.2 collective-permute-start.30
  205.8 1.6 collective-permute-done.34.rest_8_
  207.4 5.7 %collective-permute-done.30.rest_4_ = bf16[4,2,128,128]{3,2,1,0:T(8,128)(2,1)S(1)} collective-permute-done((bf16[4,2,128,128]{3,2,1,0:T(8,128)(2,1)S(1)}, bf16[4,2,128,128]{3,2,1,0:T(8,128)(2,1)S(1)}, u32[]{:S(2)}, u32[]{:S(2)}) %collective-permute-start.30) | collective-permute-done | bytes 262176 | tf_op jit(solution)/shard_map/ppermute | solution.py:779
  213.8 9.1 %project_out.1 = bf16[384,2048]{1,0:T(8,128)(2,1)} custom-call(s32[3]{0:T(128)} %copy-done.6, bf16[6,128,128]{2,1,0:T(8,128)(2,1)} %copy-done.4, bf16[6,128,128]{2,1,0:T(8,128)(2,1)} %copy-done.10, bf16[6,128,128]{2,1,0:T(8,128)(2,1)} %copy-done.11, bf16[6,128,128]{2,1,0:T(8,128)(2,1)} %copy-done.12, bf16[4,2,128,128]{3,2,1,0:T(8,128)(2,1)} %copy-done.13, ...), custom_call_target="tpu_custom_call" | custom-call | flops 3221225472 | bytes 8388608 | tf_op jit(solution)/shard_map/project_out/pallas_call | solution.py:671
  (135 shorter events, 16.8 us)
Async XLA Ops:
  6.5 206.6 %all-gather.2.cloned.1.call-start = ((), (), s32[]{:S(2)}) async-start(), calls=%async_computation | async-start | bytes 9437184 | tf_op jit(solution)/shard_map/all_gather | solution.py:766
  6.5 10.9 %collective-permute-start = (bf16[3,2048,256]{2,1,0:T(8,128)(2,1)}, bf16[3,2048,256]{2,1,0:T(8,128)(2,1)}, u32[]{:S(2)}, u32[]{:S(2)}) collective-permute-start(bf16[3,2048,256]{2,1,0:T(8,128)(2,1)} %bitcast.89), channel_id=1, source_target_pairs={{0,1},{1,0},{2,3},{3,2},{4,5},{5,4},{6,7},{7,6},{8,9},{9,8},{10,11... | collective-permute-start | bytes 9437192 | tf_op jit(solution)/shard_map/ppermute | solution.py:715
  8.8 6.3 %copy-start.5 = (s32[6,12]{1,0:T(8,128)S(1)}, s32[6,12]{1,0:T(8,128)}, u32[]{:S(2)}) copy-start(s32[6,12]{1,0:T(8,128)} %refs_0_.7) | copy-start | bytes 868
  10.4 37.7 %collective-permute-start.5 = (bf16[384,2048]{1,0:T(8,128)(2,1)}, bf16[384,2048]{1,0:T(8,128)(2,1)S(1)}, u32[]{:S(2)}, u32[]{:S(2)}) collective-permute-start(bf16[384,2048]{1,0:T(8,128)(2,1)} %fusion.2.rest_0_), channel_id=1, source_target_pairs={{0,2},{1,3},{2,0},{3,1},{4,6},{5,7},{6,4},{7,5},{8,10},{9,11},{10,... | collective-permute-start | bytes 4718600 | tf_op jit(solution)/shard_map/ppermute | solution.py:723
  13.0 36.7 %collective-permute-start.4 = (bf16[384,2048]{1,0:T(8,128)(2,1)}, bf16[384,2048]{1,0:T(8,128)(2,1)}, u32[]{:S(2)}, u32[]{:S(2)}) collective-permute-start(bf16[384,2048]{1,0:T(8,128)(2,1)} %fusion.2.rest_0_), channel_id=1, source_target_pairs={{0,4},{1,5},{2,6},{3,7},{4,0},{5,1},{6,2},{7,3},{8,12},{9,13},{10,... | collective-permute-start | bytes 4718600 | tf_op jit(solution)/shard_map/ppermute | solution.py:722
  25.3 33.1 %collective-permute-start.1 = (bf16[400,384]{1,0:T(8,128)(2,1)}, bf16[400,384]{1,0:T(8,128)(2,1)S(1)}, u32[]{:S(2)}, u32[]{:S(2)}) collective-permute-start(bf16[400,384]{1,0:T(8,128)(2,1)} %get-tuple-element.90), channel_id=1, source_target_pairs={{0,8},{8,16},{16,24},{24,0},{1,9},{9,17},{17,25},{25,1},{2,10},{10... | collective-permute-start | bytes 921608 | tf_op jit(solution)/shard_map/ppermute | solution.py:708
  27.0 31.5 %collective-permute-start.2 = (bf16[400,384]{1,0:T(8,128)(2,1)}, bf16[400,384]{1,0:T(8,128)(2,1)S(1)}, u32[]{:S(2)}, u32[]{:S(2)}) collective-permute-start(bf16[400,384]{1,0:T(8,128)(2,1)} %get-tuple-element.91), channel_id=1, source_target_pairs={{0,16},{8,24},{16,0},{24,8},{1,17},{9,25},{17,1},{25,9},{2,18},{10... | collective-permute-start | bytes 921608 | tf_op jit(solution)/shard_map/ppermute | solution.py:708
  29.6 28.9 %collective-permute-start.3 = (bf16[400,384]{1,0:T(8,128)(2,1)}, bf16[400,384]{1,0:T(8,128)(2,1)S(1)}, u32[]{:S(2)}, u32[]{:S(2)}) collective-permute-start(bf16[400,384]{1,0:T(8,128)(2,1)} %get-tuple-element.92), channel_id=1, source_target_pairs={{0,24},{8,0},{16,8},{24,16},{1,25},{9,1},{17,9},{25,17},{2,26},{10... | collective-permute-start | bytes 921608 | tf_op jit(solution)/shard_map/ppermute | solution.py:708
  58.5 19.3 %collective-permute-start.10 = (bf16[192,2048]{1,0:T(8,128)(2,1)}, bf16[192,2048]{1,0:T(8,128)(2,1)S(1)}, u32[]{:S(2)}, u32[]{:S(2)}) collective-permute-start(bf16[192,2048]{1,0:T(8,128)(2,1)} %get-tuple-element.109), channel_id=1, source_target_pairs={{0,4},{1,5},{2,6},{3,7},{4,0},{5,1},{6,2},{7,3},{8,12},{9,13},{10,... | collective-permute-start | bytes 2359304 | tf_op jit(solution)/shard_map/ppermute | solution.py:757
  60.1 18.9 %collective-permute-start.9 = (bf16[192,2048]{1,0:T(8,128)(2,1)}, bf16[192,2048]{1,0:T(8,128)(2,1)S(1)}, u32[]{:S(2)}, u32[]{:S(2)}) collective-permute-start(bf16[192,2048]{1,0:T(8,128)(2,1)} %get-tuple-element.108), channel_id=1, source_target_pairs={{0,2},{1,3},{2,0},{3,1},{4,6},{5,7},{6,4},{7,5},{8,10},{9,11},{10,... | collective-permute-start | bytes 2359304 | tf_op jit(solution)/shard_map/ppermute | solution.py:756
  62.2 26.6 %collective-permute-start.6 = (bf16[384,384]{1,0:T(8,128)(2,1)}, bf16[384,384]{1,0:T(8,128)(2,1)S(1)}, u32[]{:S(2)}, u32[]{:S(2)}) collective-permute-start(bf16[384,384]{1,0:T(8,128)(2,1)} %get-tuple-element.105), channel_id=1, source_target_pairs={{0,8},{8,16},{16,24},{24,0},{1,9},{9,17},{17,25},{25,1},{2,10},{10... | collective-permute-start | bytes 884744 | tf_op jit(solution)/shard_map/ppermute | solution.py:708
  63.8 25.0 %collective-permute-start.7 = (bf16[384,384]{1,0:T(8,128)(2,1)}, bf16[384,384]{1,0:T(8,128)(2,1)S(1)}, u32[]{:S(2)}, u32[]{:S(2)}) collective-permute-start(bf16[384,384]{1,0:T(8,128)(2,1)} %get-tuple-element.106), channel_id=1, source_target_pairs={{0,16},{8,24},{16,0},{24,8},{1,17},{9,25},{17,1},{25,9},{2,18},{10... | collective-permute-start | bytes 884744 | tf_op jit(solution)/shard_map/ppermute | solution.py:708
  66.4 22.4 %collective-permute-start.8 = (bf16[384,384]{1,0:T(8,128)(2,1)}, bf16[384,384]{1,0:T(8,128)(2,1)S(1)}, u32[]{:S(2)}, u32[]{:S(2)}) collective-permute-start(bf16[384,384]{1,0:T(8,128)(2,1)} %get-tuple-element.107), channel_id=1, source_target_pairs={{0,24},{8,0},{16,8},{24,16},{1,25},{9,1},{17,9},{25,17},{2,26},{10... | collective-permute-start | bytes 884744 | tf_op jit(solution)/shard_map/ppermute | solution.py:708
  90.5 6.4 %copy-start.1 = (bf16[384,384]{1,0:T(8,128)(2,1)S(1)}, bf16[384,384]{1,0:T(8,128)(2,1)}, u32[]{:S(2)}) copy-start(bf16[384,384]{1,0:T(8,128)(2,1)} %get-tuple-element.127.refs_8_.refs_12_) | copy-start | bytes 884740
  90.7 33.3 %collective-permute-start.17 = (bf16[4,400,384]{2,1,0:T(8,128)(2,1)S(1)}, bf16[4,400,384]{2,1,0:T(8,128)(2,1)S(1)}, u32[]{:S(2)}, u32[]{:S(2)}) collective-permute-start(bf16[4,400,384]{2,1,0:T(8,128)(2,1)S(1)} %pad_maximum_fusion), channel_id=1, source_target_pairs={{0,1},{1,0},{2,3},{3,2},{4,5},{5,4},{6,7},{7,6},{8,9},{9,8},{10,11... | collective-permute-start | bytes 3686408 | tf_op jit(solution)/shard_map/ppermute | solution.py:740
  91.5 15.8 %collective-permute-start.11 = (bf16[384,384]{1,0:T(8,128)(2,1)S(1)}, bf16[384,384]{1,0:T(8,128)(2,1)S(1)}, u32[]{:S(2)}, u32[]{:S(2)}) collective-permute-start(bf16[384,384]{1,0:T(8,128)(2,1)S(1)} %copy-done.22), channel_id=1, source_target_pairs={{0,8},{8,16},{16,24},{24,0},{1,9},{9,17},{17,25},{25,1},{2,10},{10... | collective-permute-start | bytes 884744 | tf_op jit(solution)/shard_map/ppermute | solution.py:708
  94.5 20.8 %collective-permute-start.12 = (bf16[384,384]{1,0:T(8,128)(2,1)S(1)}, bf16[384,384]{1,0:T(8,128)(2,1)S(1)}, u32[]{:S(2)}, u32[]{:S(2)}) collective-permute-start(bf16[384,384]{1,0:T(8,128)(2,1)S(1)} %copy-done.20), channel_id=1, source_target_pairs={{0,16},{8,24},{16,0},{24,8},{1,17},{9,25},{17,1},{25,9},{2,18},{10... | collective-permute-start | bytes 884744 | tf_op jit(solution)/shard_map/ppermute | solution.py:708
  96.1 19.2 %collective-permute-start.13 = (bf16[384,384]{1,0:T(8,128)(2,1)S(1)}, bf16[384,384]{1,0:T(8,128)(2,1)S(1)}, u32[]{:S(2)}, u32[]{:S(2)}) collective-permute-start(bf16[384,384]{1,0:T(8,128)(2,1)S(1)} %copy-done.19), channel_id=1, source_target_pairs={{0,24},{8,0},{16,8},{24,16},{1,25},{9,1},{17,9},{25,17},{2,26},{10... | collective-permute-start | bytes 884744 | tf_op jit(solution)/shard_map/ppermute | solution.py:708
  98.1 17.1 %copy-start.2 = (bf16[384,384]{1,0:T(8,128)(2,1)S(1)}, bf16[384,384]{1,0:T(8,128)(2,1)}, u32[]{:S(2)}) copy-start(bf16[384,384]{1,0:T(8,128)(2,1)} %get-tuple-element.131.refs_12_.refs_16_) | copy-start | bytes 884740
  98.1 26.9 %collective-permute-start.18 = (bf16[4,384,384]{2,1,0:T(8,128)(2,1)}, bf16[4,384,384]{2,1,0:T(8,128)(2,1)S(1)}, u32[]{:S(2)}, u32[]{:S(2)}) collective-permute-start(bf16[4,384,384]{2,1,0:T(8,128)(2,1)} %pad_maximum_fusion.1), channel_id=1, source_target_pairs={{0,1},{1,0},{2,3},{3,2},{4,5},{5,4},{6,7},{7,6},{8,9},{9,8},{10,11... | collective-permute-start | bytes 3538952 | tf_op jit(solution)/shard_map/ppermute | solution.py:740
  107.2 8.4 %copy-start.24 = (bf16[384,384]{1,0:T(8,128)(2,1)S(1)}, bf16[384,384]{1,0:T(8,128)(2,1)}, u32[]{:S(2)}) copy-start(bf16[384,384]{1,0:T(8,128)(2,1)} %get-tuple-element.124) | copy-start | bytes 884740
  107.2 15.4 %copy-start.23 = (bf16[384,384]{1,0:T(8,128)(2,1)S(1)}, bf16[384,384]{1,0:T(8,128)(2,1)}, u32[]{:S(2)}) copy-start(bf16[384,384]{1,0:T(8,128)(2,1)} %get-tuple-element.125) | copy-start | bytes 884740
  107.2 16.8 %copy-start.21 = (bf16[384,384]{1,0:T(8,128)(2,1)S(1)}, bf16[384,384]{1,0:T(8,128)(2,1)}, u32[]{:S(2)}) copy-start(bf16[384,384]{1,0:T(8,128)(2,1)} %get-tuple-element.126) | copy-start | bytes 884740
  115.5 9.6 %collective-permute-start.19 = (bf16[4,384,384]{2,1,0:T(8,128)(2,1)S(1)}, bf16[4,384,384]{2,1,0:T(8,128)(2,1)S(1)}, u32[]{:S(2)}, u32[]{:S(2)}) collective-permute-start(bf16[4,384,384]{2,1,0:T(8,128)(2,1)S(1)} %pad_maximum_fusion.2), channel_id=1, source_target_pairs={{0,1},{1,0},{2,3},{3,2},{4,5},{5,4},{6,7},{7,6},{8,9},{9,8},{10,11... | collective-permute-start | bytes 3538952 | tf_op jit(solution)/shard_map/ppermute | solution.py:740
  115.6 73.6 %copy-start.6 = (s32[3]{0:T(128)}, s32[3]{0:T(128)S(1)}, u32[]{:S(2)}) copy-start(s32[3]{0:T(128)S(1)} %pad_add_fusion.place) | copy-start | bytes 40
  115.6 27.0 %collective-permute-start.14 = (bf16[384,384]{1,0:T(8,128)(2,1)S(1)}, bf16[384,384]{1,0:T(8,128)(2,1)S(1)}, u32[]{:S(2)}, u32[]{:S(2)}) collective-permute-start(bf16[384,384]{1,0:T(8,128)(2,1)S(1)} %copy-done.24), channel_id=1, source_target_pairs={{0,8},{8,16},{16,24},{24,0},{1,9},{9,17},{17,25},{25,1},{2,10},{10... | collective-permute-start | bytes 884744 | tf_op jit(solution)/shard_map/ppermute | solution.py:708
  122.6 21.2 %collective-permute-start.15 = (bf16[384,384]{1,0:T(8,128)(2,1)S(1)}, bf16[384,384]{1,0:T(8,128)(2,1)S(1)}, u32[]{:S(2)}, u32[]{:S(2)}) collective-permute-start(bf16[384,384]{1,0:T(8,128)(2,1)S(1)} %copy-done.23), channel_id=1, source_target_pairs={{0,16},{8,24},{16,0},{24,8},{1,17},{9,25},{17,1},{25,9},{2,18},{10... | collective-permute-start | bytes 884744 | tf_op jit(solution)/shard_map/ppermute | solution.py:708
  124.0 19.9 %collective-permute-start.16 = (bf16[384,384]{1,0:T(8,128)(2,1)S(1)}, bf16[384,384]{1,0:T(8,128)(2,1)S(1)}, u32[]{:S(2)}, u32[]{:S(2)}) collective-permute-start(bf16[384,384]{1,0:T(8,128)(2,1)S(1)} %copy-done.21), channel_id=1, source_target_pairs={{0,24},{8,0},{16,8},{24,16},{1,25},{9,1},{17,9},{25,17},{2,26},{10... | collective-permute-start | bytes 884744 | tf_op jit(solution)/shard_map/ppermute | solution.py:708
  125.1 18.8 %copy-start.3 = (bf16[384,384]{1,0:T(8,128)(2,1)S(1)}, bf16[384,384]{1,0:T(8,128)(2,1)}, u32[]{:S(2)}) copy-start(bf16[384,384]{1,0:T(8,128)(2,1)} %get-tuple-element.138.refs_8_) | copy-start | bytes 884740
  143.8 1.6 collective-permute-start.20
  143.9 2.0 collective-permute-start.21
  144.4 1.9 collective-permute-start.22
  144.4 2.3 collective-permute-start.23
  157.6 24.8 %collective-permute-start.24 = (bf16[6,128,128]{2,1,0:T(8,128)(2,1)S(1)}, bf16[6,128,128]{2,1,0:T(8,128)(2,1)S(1)}, u32[]{:S(2)}, u32[]{:S(2)}) collective-permute-start(bf16[6,128,128]{2,1,0:T(8,128)(2,1)S(1)} %get-tuple-element.149), channel_id=1, source_target_pairs={{0,8},{8,16},{16,24},{24,0},{1,9},{9,17},{17,25},{25,1},{2,10},{10... | collective-permute-start | bytes 589832 | tf_op jit(solution)/shard_map/ppermute | solution.py:708
  164.4 18.0 %collective-permute-start.25 = (bf16[6,128,128]{2,1,0:T(8,128)(2,1)S(1)}, bf16[6,128,128]{2,1,0:T(8,128)(2,1)S(1)}, u32[]{:S(2)}, u32[]{:S(2)}) collective-permute-start(bf16[6,128,128]{2,1,0:T(8,128)(2,1)S(1)} %get-tuple-element.150), channel_id=1, source_target_pairs={{0,16},{8,24},{16,0},{24,8},{1,17},{9,25},{17,1},{25,9},{2,18},{10... | collective-permute-start | bytes 589832 | tf_op jit(solution)/shard_map/ppermute | solution.py:708
  165.8 16.6 %collective-permute-start.26 = (bf16[6,128,128]{2,1,0:T(8,128)(2,1)S(1)}, bf16[6,128,128]{2,1,0:T(8,128)(2,1)S(1)}, u32[]{:S(2)}, u32[]{:S(2)}) collective-permute-start(bf16[6,128,128]{2,1,0:T(8,128)(2,1)S(1)} %get-tuple-element.151), channel_id=1, source_target_pairs={{0,24},{8,0},{16,8},{24,16},{1,25},{9,1},{17,9},{25,17},{2,26},{10... | collective-permute-start | bytes 589832 | tf_op jit(solution)/shard_map/ppermute | solution.py:708
  182.6 19.6 %collective-permute-start.32 = (bf16[4,3,128,128]{3,2,0,1:T(8,128)(2,1)S(1)}, bf16[4,3,128,128]{3,2,0,1:T(8,128)(2,1)S(1)}, u32[]{:S(2)}, u32[]{:S(2)}) collective-permute-start(bf16[4,3,128,128]{3,2,0,1:T(8,128)(2,1)S(1)} %pad_maximum_fusion.4), channel_id=1, source_target_pairs={{0,6},{1,7},{2,4},{3,5},{4,2},{5,3},{6,0},{7,1},{8,14},{9,15},{10,... | collective-permute-start | bytes 1179656 | tf_op jit(solution)/shard_map/ppermute | solution.py:779
  183.7 18.8 %collective-permute-start.31 = (bf16[4,3,128,128]{3,2,1,0:T(8,128)(2,1)S(1)}, bf16[4,3,128,128]{3,2,1,0:T(8,128)(2,1)S(1)}, u32[]{:S(2)}, u32[]{:S(2)}) collective-permute-start(bf16[4,3,128,128]{3,2,1,0:T(8,128)(2,1)S(1)} %pad_maximum_fusion.3), channel_id=1, source_target_pairs={{0,4},{1,5},{2,6},{3,7},{4,0},{5,1},{6,2},{7,3},{8,12},{9,13},{10,... | collective-permute-start | bytes 1179656 | tf_op jit(solution)/shard_map/ppermute | solution.py:779
  185.3 9.8 %collective-permute-start.27 = (bf16[6,128,128]{2,1,0:T(8,128)(2,1)S(1)}, bf16[6,128,128]{2,1,0:T(8,128)(2,1)S(1)}, u32[]{:S(2)}, u32[]{:S(2)}) collective-permute-start(bf16[6,128,128]{2,1,0:T(8,128)(2,1)S(1)} %get-tuple-element.153), channel_id=1, source_target_pairs={{0,8},{8,16},{16,24},{24,0},{1,9},{9,17},{17,25},{25,1},{2,10},{10... | collective-permute-start | bytes 589832 | tf_op jit(solution)/shard_map/ppermute | solution.py:708
  186.5 15.0 %collective-permute-start.28 = (bf16[6,128,128]{2,1,0:T(8,128)(2,1)S(1)}, bf16[6,128,128]{2,1,0:T(8,128)(2,1)S(1)}, u32[]{:S(2)}, u32[]{:S(2)}) collective-permute-start(bf16[6,128,128]{2,1,0:T(8,128)(2,1)S(1)} %get-tuple-element.154), channel_id=1, source_target_pairs={{0,16},{8,24},{16,0},{24,8},{1,17},{9,25},{17,1},{25,9},{2,18},{10... | collective-permute-start | bytes 589832 | tf_op jit(solution)/shard_map/ppermute | solution.py:708
  188.1 13.5 %collective-permute-start.29 = (bf16[6,128,128]{2,1,0:T(8,128)(2,1)S(1)}, bf16[6,128,128]{2,1,0:T(8,128)(2,1)S(1)}, u32[]{:S(2)}, u32[]{:S(2)}) collective-permute-start(bf16[6,128,128]{2,1,0:T(8,128)(2,1)S(1)} %get-tuple-element.155), channel_id=1, source_target_pairs={{0,24},{8,0},{16,8},{24,16},{1,25},{9,1},{17,9},{25,17},{2,26},{10... | collective-permute-start | bytes 589832 | tf_op jit(solution)/shard_map/ppermute | solution.py:708
  194.6 8.4 %copy-start.4 = (bf16[6,128,128]{2,1,0:T(8,128)(2,1)}, bf16[6,128,128]{2,1,0:T(8,128)(2,1)S(1)}, u32[]{:S(2)}) copy-start(bf16[6,128,128]{2,1,0:T(8,128)(2,1)S(1)} %attend_local.1.rest_0_) | copy-start | bytes 589828
  195.1 7.8 %copy-start.10 = (bf16[6,128,128]{2,1,0:T(8,128)(2,1)}, bf16[6,128,128]{2,1,0:T(8,128)(2,1)S(1)}, u32[]{:S(2)}) copy-start(bf16[6,128,128]{2,1,0:T(8,128)(2,1)S(1)} %collective-permute-done.27.rest_1_) | copy-start | bytes 589828
  201.6 5.8 %collective-permute-start.34 = (bf16[4,1,128,128]{3,2,1,0:T(8,128)(2,1)S(1)}, bf16[4,1,128,128]{3,2,1,0:T(8,128)(2,1)S(1)}, u32[]{:S(2)}, u32[]{:S(2)}) collective-permute-start(bf16[4,1,128,128]{3,2,1,0:T(8,128)(2,1)S(1)} %pad_maximum_fusion.16), channel_id=1, source_target_pairs={{0,3},{1,2},{2,1},{3,0},{4,7},{5,6},{6,5},{7,4},{8,11},{9,10},{10,... | collective-permute-start | bytes 393224 | tf_op jit(solution)/shard_map/ppermute | solution.py:779
  202.6 2.5 %collective-permute-start.35 = (bf16[2,4,1,128,128]{4,3,1,2,0:T(8,128)(2,1)S(1)}, bf16[2,4,1,128,128]{4,3,1,2,0:T(8,128)(2,1)S(1)}, u32[]{:S(2)}, u32[]{:S(2)}) collective-permute-start(bf16[2,4,1,128,128]{4,3,1,2,0:T(8,128)(2,1)S(1)} %pad_maximum_fusion.6), channel_id=1, source_target_pairs={{0,1},{1,0},{2,3},{3,2},{4,5},{5,4},{6,7},{7,6},{8,9},{9,8},{10,11... | collective-permute-start | bytes 786440 | tf_op jit(solution)/shard_map/ppermute | solution.py:740
  203.0 10.1 %collective-permute-start.30 = (bf16[4,2,128,128]{3,2,1,0:T(8,128)(2,1)S(1)}, bf16[4,2,128,128]{3,2,1,0:T(8,128)(2,1)S(1)}, u32[]{:S(2)}, u32[]{:S(2)}) collective-permute-start(bf16[4,2,128,128]{3,2,1,0:T(8,128)(2,1)S(1)} %pad_maximum_fusion.5), channel_id=1, source_target_pairs={{0,2},{1,3},{2,0},{3,1},{4,6},{5,7},{6,4},{7,5},{8,10},{9,11},{10,... | collective-permute-start | bytes 786440 | tf_op jit(solution)/shard_map/ppermute | solution.py:779
  204.2 3.2 %collective-permute-start.33 = (bf16[4,1,128,128]{3,2,1,0:T(8,128)(2,1)S(1)}, bf16[4,1,128,128]{3,2,1,0:T(8,128)(2,1)S(1)}, u32[]{:S(2)}, u32[]{:S(2)}) collective-permute-start(bf16[4,1,128,128]{3,2,1,0:T(8,128)(2,1)S(1)} %pad_maximum_fusion.15), channel_id=1, source_target_pairs={{0,1},{1,0},{2,3},{3,2},{4,5},{5,4},{6,7},{7,6},{8,9},{9,8},{10,11... | collective-permute-start | bytes 393224 | tf_op jit(solution)/shard_map/ppermute | solution.py:740
  207.4 5.7 %copy-start.14 = (bf16[4,1,128,128]{3,2,1,0:T(8,128)(2,1)}, bf16[4,1,128,128]{3,2,1,0:T(8,128)(2,1)S(1)}, u32[]{:S(2)}) copy-start(bf16[4,1,128,128]{3,2,1,0:T(8,128)(2,1)S(1)} %collective-permute-done.34.rest_8_) | copy-start | bytes 393220
  (14 other events, 33.5 us)
Sparse Core Ops, SparseCore 0:
  89.0 55.2 all-gather.1
